TPU v7x, 512 devices: a whole 4x4x16 slice. The times are simulated.
512 devices in a mesh: section: 8 (over x, core), expert: 8 (over z_lo), dp: 8 (over y, z_hi).
Axes of the slice: x: 4, y: 4, z: 16 (z_hi: 2, z_lo: 8; z = z_hi * 8 + z_lo), core: 2. Of those that a mesh axis runs over, the one named last changes fastest.
Arguments:
- layer_input: bfloat16 [8, 8192, 2048], P('section', ('expert', 'dp')), may hold values from -6 to 6
- output_grad: bfloat16 [8, 8192, 2048], P('section', ('expert', 'dp')), may hold values from -6 to 6
- expert_ids: int32 [8, 8192], P('section', ('expert', 'dp')), may hold values from 0 to 63, as said below
- w_gate: bfloat16 [8, 2048, 8192], P('section', None, ('expert', 'dp')), may hold values from -0.125 to 0.125
- w_up: bfloat16 [8, 2048, 8192], P('section', None, ('expert', 'dp')), may hold values from -0.125 to 0.125
- w_down: bfloat16 [8, 2048, 8192], P('section', None, ('expert', 'dp')), may hold values from -0.0625 to 0.0625
Outputs:
- input_grad: bfloat16 [8, 8192, 2048], P('section', ('expert', 'dp'))
- grad_gate: bfloat16 [8, 2048, 8192], P('section', None, ('expert', 'dp'))
- grad_up: bfloat16 [8, 2048, 8192], P('section', None, ('expert', 'dp'))
- grad_down: bfloat16 [8, 2048, 8192], P('section', None, ('expert', 'dp'))
Inputs may be any that keep to these rules, and one draw needn't show every extreme that they name: `expert_ids`: expert 0 is the expert of these weights. Every device's 128 tokens name expert 0 between 1 and 8 times, and on every section some device names it exactly 8 times.
All inputs are finite; a program needn't handle non-finite values.
Results may differ from a plain program's by a relative error of at most 0.0065.
Values may be sent and summed in bfloat16 or wider, within the bound.
A program may use at most 64 MiB of HBM per device.

v0:
```python
import jax
import jax.numpy as jnp
from jax import lax
from jax.sharding import PartitionSpec as P

SLOT = 8


def shifted(value, axis, steps):
    count = lax.axis_size(axis)
    pairs = [(source, (source + steps) % count) for source in range(count)]
    return lax.ppermute(value, axis, pairs)


def unit_grads(x_rows, dy_rows, w_gate, w_up, w_down):
    gate = jnp.dot(x_rows, w_gate, preferred_element_type=jnp.float32)
    upper = jnp.dot(x_rows, w_up, preferred_element_type=jnp.float32)
    sigma = jax.nn.sigmoid(gate)
    active = gate * sigma
    hidden = (active * upper).astype(jnp.bfloat16)
    d_hidden = jnp.dot(dy_rows, w_down, preferred_element_type=jnp.float32)
    d_gate = (d_hidden * upper * sigma * (1.0 + gate * (1.0 - sigma))).astype(jnp.bfloat16)
    d_up = (d_hidden * active).astype(jnp.bfloat16)
    back_dims = (((1,), (1,)), ((), ()))
    d_input = lax.dot_general(d_gate, w_gate, back_dims, preferred_element_type=jnp.float32)
    d_input = d_input + lax.dot_general(d_up, w_up, back_dims, preferred_element_type=jnp.float32)
    return (d_input, d_gate, d_up, hidden)


def weight_grads(x_rows, dy_rows, d_gate, d_up, hidden):
    row_dims = (((0,), (0,)), ((), ()))
    part_gate = lax.dot_general(x_rows, d_gate, row_dims, preferred_element_type=jnp.float32)
    part_up = lax.dot_general(x_rows, d_up, row_dims, preferred_element_type=jnp.float32)
    part_down = lax.dot_general(dy_rows, hidden, row_dims, preferred_element_type=jnp.float32)
    return (part_gate, part_up, part_down)


def body(layer_input, output_grad, expert_ids, w_gate, w_up, w_down):
    inputs = layer_input[0]
    grads = output_grad[0]
    routes = expert_ids[0]
    chosen = (routes == 0).astype(jnp.int32)
    within = jnp.cumsum(chosen) - chosen
    target = jnp.where(chosen > 0, within, SLOT)
    places = jnp.arange(SLOT, dtype=jnp.int32)
    match = (target[None, :] == places[:, None]).astype(jnp.bfloat16)
    send_x = jnp.dot(match, inputs, preferred_element_type=jnp.float32).astype(jnp.bfloat16)
    send_dy = jnp.dot(match, grads, preferred_element_type=jnp.float32).astype(jnp.bfloat16)
    group_x, group_dy = (
        lax.all_gather(send_x, "expert", axis=0, tiled=True),
        lax.all_gather(send_dy, "expert", axis=0, tiled=True),
    )
    full_gate, full_up, full_down = (
        lax.all_gather(w_gate[0], "dp", axis=1, tiled=True),
        lax.all_gather(w_up[0], "dp", axis=1, tiled=True),
        lax.all_gather(w_down[0], "dp", axis=1, tiled=True),
    )
    d_part, d_gate, d_up, hidden = unit_grads(group_x, group_dy, full_gate, full_up, full_down)
    mine = lax.psum_scatter(d_part.astype(jnp.bfloat16), "expert", scatter_dimension=0, tiled=True)
    own_gate, own_up, own_hidden = (
        lax.all_to_all(d_gate, "dp", split_axis=1, concat_axis=0, tiled=True),
        lax.all_to_all(d_up, "dp", split_axis=1, concat_axis=0, tiled=True),
        lax.all_to_all(hidden, "dp", split_axis=1, concat_axis=0, tiled=True),
    )
    every_x, every_dy = (
        lax.all_gather(group_x, "dp", axis=0, tiled=True),
        lax.all_gather(group_dy, "dp", axis=0, tiled=True),
    )
    part_gate, part_up, part_down = weight_grads(every_x, every_dy, own_gate, own_up, own_hidden)
    d_rows = lax.optimization_barrier(mine)
    term = lax.dot_general(
        match, d_rows, (((0,), (0,)), ((), ())), preferred_element_type=jnp.float32
    )
    token_grad = (grads.astype(jnp.float32) + term).astype(jnp.bfloat16)
    moved = shifted(token_grad, "section", -1)
    return (
        moved[None],
        part_gate.astype(jnp.bfloat16)[None],
        part_up.astype(jnp.bfloat16)[None],
        part_down.astype(jnp.bfloat16)[None],
    )


def solution(mesh):
    in_specs = (
        P("section", ("expert", "dp"), None),
        P("section", ("expert", "dp"), None),
        P("section", ("expert", "dp")),
        P("section", None, ("expert", "dp")),
        P("section", None, ("expert", "dp")),
        P("section", None, ("expert", "dp")),
    )
    out_specs = (
        P("section", ("expert", "dp"), None),
        P("section", None, ("expert", "dp")),
        P("section", None, ("expert", "dp")),
        P("section", None, ("expert", "dp")),
    )
    return jax.shard_map(body, mesh=mesh, in_specs=in_specs, out_specs=out_specs, check_vma=False)
```

profile of v0, /device:TPU:1, one launch (start us, length us, event | category | flops | bytes accessed | tf_op | source)
XLA Modules:
  0.0 865.0 jit_solution(5704412352356924403)
XLA Ops:
  7.2 0.0 copy-start
  7.2 0.0 all-gather.17.cloned.1.call-start
  7.2 0.7 all-gather.17.cloned.1.call-update
  7.9 0.0 all-gather.15.cloned.1.call-start
  8.0 0.7 all-gather.15.cloned.1.call-update
  8.7 0.0 all-gather.13.cloned.1.call-start
  8.7 0.7 all-gather.13.cloned.1.call-update
  9.4 0.0 reduce-scatter.2.cloned.1.call-start
  9.4 0.7 compare_convert_fusion
  10.1 0.3 reduce-window_clone.1
  10.4 0.7 fusion.27
  11.1 0.2 convolution_convert_fusion.3
  11.3 54.5 %all_gather.23 = bf16[64,2048]{1,0:T(8,128)(2,1)S(1)} all-gather(bf16[8,2048]{1,0:T(8,128)(2,1)S(1)} %convolution_convert_fusion.3), channel_id=1, replica_groups=mesh['section'=8,'expert'=8,'dp'=8] {'expert'}, dimensions={0}, use_global_device_ids=true | all-gather | bytes 294912 | tf_op jit(solution)/shard_map/all_gather | solution.py:50
  65.7 1.3 convolution_convert_fusion.4
  67.0 50.5 %all_gather.21 = bf16[64,2048]{1,0:T(8,128)(2,1)S(1)} all-gather(bf16[8,2048]{1,0:T(8,128)(2,1)S(1)} %convolution_convert_fusion.4), channel_id=1, replica_groups=mesh['section'=8,'expert'=8,'dp'=8] {'expert'}, dimensions={0}, use_global_device_ids=true | all-gather | bytes 294912 | tf_op jit(solution)/shard_map/all_gather | solution.py:51
  117.5 86.6 %all-gather.17.cloned.1.call-done = bf16[1,2048,1024]{2,1,0:T(8,128)(2,1)} async-done(((bf16[1,2048,128]{2,1,0:T(8,128)(2,1)}), bf16[1,2048,1024]{2,1,0:T(8,128)(2,1)}) %all-gather.17.cloned.1.call-update) | async-done | bytes 4194320 | tf_op jit(solution)/shard_map/all_gather | solution.py:54
  204.1 3.0 fusion.2
  207.1 175.1 %all-gather.15.cloned.1.call-done = bf16[1,2048,1024]{2,1,0:T(8,128)(2,1)} async-done(((bf16[1,2048,128]{2,1,0:T(8,128)(2,1)}), bf16[1,2048,1024]{2,1,0:T(8,128)(2,1)}) %all-gather.15.cloned.1.call-update) | async-done | bytes 4194320 | tf_op jit(solution)/shard_map/all_gather | solution.py:55
  382.2 3.0 fusion.6
  385.3 175.2 %all-gather.13.cloned.1.call-done = bf16[1,2048,1024]{2,1,0:T(8,128)(2,1)} async-done(((bf16[1,2048,128]{2,1,0:T(8,128)(2,1)}), bf16[1,2048,1024]{2,1,0:T(8,128)(2,1)}) %all-gather.13.cloned.1.call-update) | async-done | bytes 4194320 | tf_op jit(solution)/shard_map/all_gather | solution.py:56
  560.4 3.2 fusion.23
  563.7 0.2 copy-done.2
  563.9 1.4 fusion
  565.3 0.0 copy-start.6
  565.3 2.1 fusion.17
  567.4 0.0 reduce-scatter.2.cloned.1.call-update
  567.4 0.0 all-gather.9.cloned.1.call-start
  567.5 0.5 all-gather.9.cloned.1.call-update
  568.0 0.0 all-gather.11.cloned.1.call-start
  568.1 0.5 all-gather.11.cloned.1.call-update
  568.6 0.7 copy_bitcast_fusion.2
  569.3 3.4 all-to-all-start
  572.7 0.7 copy_bitcast_fusion.1
  573.4 13.7 %all-to-all-done = bf16[64,8,128]{2,0,1:T(8,128)(2,1)S(1)} async-done(((bf16[64,8,128]{2,0,1:T(8,128)(2,1)}), bf16[64,8,128]{2,0,1:T(8,128)(2,1)S(1)}, u32[]{:S(2)}, u32[]{:S(2)}) %all-to-all-start) | async-done | bytes 131104 | tf_op jit(solution)/shard_map/all_to_all | solution.py:61
  587.1 3.4 all-to-all-start.1
  590.5 0.7 copy.19
  591.2 28.4 %reduce-scatter.2.cloned.1.call-done = bf16[8,2048]{1,0:T(8,128)(2,1)} async-done(((bf16[64,2048]{1,0:T(8,128)(2,1)}), bf16[8,2048]{1,0:T(8,128)(2,1)}) %reduce-scatter.2.cloned.1.call-update) | async-done | bytes 32784 | tf_op jit(solution)/shard_map/reduce_scatter | solution.py:59
  619.6 0.0 all-to-all-done.1
  619.6 7.4 all-to-all-start.2
  627.0 1.1 fusion.10
  628.1 4.8 collective-permute-start
  633.0 105.9 %all-gather.9.cloned.1.call-done = bf16[512,2048]{1,0:T(8,128)(2,1)} async-done(((bf16[64,2048]{1,0:T(8,128)(2,1)}), bf16[512,2048]{1,0:T(8,128)(2,1)}) %all-gather.9.cloned.1.call-update) | async-done | bytes 2097168 | tf_op jit(solution)/shard_map/all_gather | solution.py:66
  738.8 3.3 fusion.14
  742.1 1.6 fusion.15
  743.7 110.6 %all-gather.11.cloned.1.call-done = bf16[512,2048]{1,0:T(8,128)(2,1)} async-done(((bf16[64,2048]{1,0:T(8,128)(2,1)}), bf16[512,2048]{1,0:T(8,128)(2,1)}) %all-gather.11.cloned.1.call-update) | async-done | bytes 2097168 | tf_op jit(solution)/shard_map/all_gather | solution.py:67
  854.2 0.0 all-to-all-done.2
  854.2 3.1 fusion.16
  857.4 0.8 copy.21
  (12 shorter events, 0.0 us)
Async XLA Ops:
  7.2 3.9 copy-start
  7.2 196.9 %all-gather.17.cloned.1.call-start = ((), (), s32[]{:S(2)}) async-start(), calls=%async_computation.9 | async-start | bytes 4718592 | tf_op jit(solution)/shard_map/all_gather | solution.py:54
  7.9 374.3 %all-gather.15.cloned.1.call-start = ((), (), s32[]{:S(2)}) async-start(), calls=%async_computation.8 | async-start | bytes 4718592 | tf_op jit(solution)/shard_map/all_gather | solution.py:55
  8.7 551.8 %all-gather.13.cloned.1.call-start = ((), (), s32[]{:S(2)}) async-start(), calls=%async_computation.7 | async-start | bytes 4718592 | tf_op jit(solution)/shard_map/all_gather | solution.py:56
  9.4 610.2 %reduce-scatter.2.cloned.1.call-start = ((), (), s32[]{:S(2)}) async-start(), calls=%async_computation.4 | async-start | bytes 294912 | tf_op jit(solution)/shard_map/reduce_scatter | solution.py:59
  65.7 319.6 %copy-start.4 = (bf16[64,2048]{1,0:T(8,128)(2,1)}, bf16[64,2048]{1,0:T(8,128)(2,1)S(1)}, u32[]{:S(2)}) copy-start(bf16[64,2048]{1,0:T(8,128)(2,1)S(1)} %all_gather.23) | copy-start | bytes 786436
  117.5 442.9 %copy-start.5 = (bf16[64,2048]{1,0:T(8,128)(2,1)}, bf16[64,2048]{1,0:T(8,128)(2,1)S(1)}, u32[]{:S(2)}) copy-start(bf16[64,2048]{1,0:T(8,128)(2,1)S(1)} %all_gather.21) | copy-start | bytes 786436
  560.4 3.4 copy-start.2
  560.4 4.8 copy-start.3
  565.3 61.8 %copy-start.6 = (bf16[1,128,2048]{2,1,0:T(8,128)(2,1)S(1)}, bf16[1,128,2048]{2,1,0:T(8,128)(2,1)}, u32[]{:S(2)}) copy-start(bf16[1,128,2048]{2,1,0:T(8,128)(2,1)} %param.7) | copy-start | bytes 1572868
  567.4 171.4 %all-gather.9.cloned.1.call-start = ((), (), s32[]{:S(2)}) async-start(), calls=%async_computation.5 | async-start | bytes 2359296 | tf_op jit(solution)/shard_map/all_gather | solution.py:66
  568.0 286.2 %all-gather.11.cloned.1.call-start = ((), (), s32[]{:S(2)}) async-start(), calls=%async_computation.6 | async-start | bytes 2359296 | tf_op jit(solution)/shard_map/all_gather | solution.py:67
  569.3 17.8 %all-to-all-start = ((bf16[64,8,128]{2,0,1:T(8,128)(2,1)}), bf16[64,8,128]{2,0,1:T(8,128)(2,1)S(1)}, u32[]{:S(2)}, u32[]{:S(2)}) async-start(bf16[64,8,128]{2,0,1:T(8,128)(2,1)} %copy_bitcast_fusion.2), calls=%async_computation.1 | async-start | bytes 262144 | tf_op jit(solution)/shard_map/all_to_all | solution.py:61
  587.1 32.5 %all-to-all-start.1 = ((bf16[64,8,128]{2,0,1:T(8,128)(2,1)}), bf16[64,8,128]{2,0,1:T(8,128)(2,1)S(1)}, u32[]{:S(2)}, u32[]{:S(2)}) async-start(bf16[64,8,128]{2,0,1:T(8,128)(2,1)} %copy_bitcast_fusion.1), calls=%async_computation.2 | async-start | bytes 262144 | tf_op jit(solution)/shard_map/all_to_all | solution.py:62
  619.6 234.6 %all-to-all-start.2 = ((bf16[64,8,128]{2,0,1:T(8,128)(2,1)}), bf16[64,8,128]{2,0,1:T(8,128)(2,1)S(1)}, u32[]{:S(2)}, u32[]{:S(2)}) async-start(bf16[64,8,128]{2,0,1:T(8,128)(2,1)} %bitcast.70), calls=%async_computation.3 | async-start | bytes 262144 | tf_op jit(solution)/shard_map/all_to_all | solution.py:63
  628.1 229.2 %collective-permute-start = (bf16[128,2048]{1,0:T(8,128)(2,1)S(1)}, bf16[128,2048]{1,0:T(8,128)(2,1)S(1)}, u32[]{:S(2)}, u32[]{:S(2)}) collective-permute-start(bf16[128,2048]{1,0:T(8,128)(2,1)S(1)} %fusion.10), channel_id=1, source_target_pairs={{0,448},{64,0},{128,64},{192,128},{256,192},{320,256},{384,320},{4... | collective-permute-start | bytes 1572872 | tf_op jit(solution)/shard_map/ppermute | solution.py:12
  738.8 3.3 copy-start.1
Sparse Core Ops, SparseCore 0:
  11.1 192.9 all-gather.16
  207.2 175.0 all-gather.14
  385.3 175.0 all-gather.12
  567.5 52.0 reduce-scatter.1
  623.7 115.0 all-gather.8
  742.9 111.2 all-gather.10
where the time goes:
time: 866 us; the launch traced here: 865 us
  waiting for transfers between devices  699 us (81%)
  blocking collectives  105 us (12%)
  matrix products  23.4 us (3%)
  starting transfers between devices  19.3 us (2%)
  between operations  14.2 us (2%)
    all_gather x1, waiting for transfers between devices, body(): lax.all_gather(w_down[0], 'dp', axis=1, tiled=True)  175 us
    all_gather x1, waiting for transfers between devices, body(): lax.all_gather(w_up[0], 'dp', axis=1, tiled=True)  175 us
    all_gather x1, waiting for transfers between devices, body(): lax.all_gather(group_dy, 'dp', axis=0, tiled=True)  111 us
    all_gather x1, waiting for transfers between devices, body(): lax.all_gather(group_x, 'dp', axis=0, tiled=True)  106 us
    all_gather x1, waiting for transfers between devices, body(): lax.all_gather(w_gate[0], 'dp', axis=1, tiled=True)  86.6 us
    all_gather x1, blocking collectives, body(): lax.all_gather(send_x, 'expert', axis=0, tiled=True)  54.5 us
    all_gather x1, blocking collectives, body(): lax.all_gather(send_dy, 'expert', axis=0, tiled=True)  50.5 us
    reduce_scatter x1, waiting for transfers between devices, body(): lax.psum_scatter(d_part.astype(jnp.bfloat16), 'expert', scatter_dimension...  28.4 us
  transfers between devices with their start and end apart: 10, of which 7 were waited for; matrix products, arithmetic and copies ran while one was open for 2% of the time, Pallas kernels for 0%

commit v1 on v0

--- a/solution.py
+++ b/solution.py
@@ -40,7 +40,8 @@
     grads = output_grad[0]
     routes = expert_ids[0]
     chosen = (routes == 0).astype(jnp.int32)
-    within = jnp.cumsum(chosen) - chosen
+    order = jnp.arange(chosen.shape[0], dtype=jnp.int32)
+    within = jnp.sum(jnp.where(order[None, :] < order[:, None], chosen[None, :], 0), axis=1)
     target = jnp.where(chosen > 0, within, SLOT)
     places = jnp.arange(SLOT, dtype=jnp.int32)
     match = (target[None, :] == places[:, None]).astype(jnp.bfloat16)

time: 866 us -> 866 us (level)
  no operation moved by 1% of the time
where the time goes in v1:
time: 866 us; the launch traced here: 865 us
  waiting for transfers between devices  698 us (81%)
  blocking collectives  106 us (12%)
  matrix products  23.4 us (3%)
  starting transfers between devices  19.3 us (2%)
  between operations  14.2 us (2%)
    all_gather x1, waiting for transfers between devices, body(): lax.all_gather(w_down[0], 'dp', axis=1, tiled=True)  175 us
    all_gather x1, waiting for transfers between devices, body(): lax.all_gather(w_up[0], 'dp', axis=1, tiled=True)  175 us
    all_gather x1, waiting for transfers between devices, body(): lax.all_gather(group_dy, 'dp', axis=0, tiled=True)  111 us
    all_gather x1, waiting for transfers between devices, body(): lax.all_gather(group_x, 'dp', axis=0, tiled=True)  106 us
    all_gather x1, waiting for transfers between devices, body(): lax.all_gather(w_gate[0], 'dp', axis=1, tiled=True)  85.7 us
    all_gather x1, blocking collectives, body(): lax.all_gather(send_x, 'expert', axis=0, tiled=True)  54.4 us
    all_gather x1, blocking collectives, body(): lax.all_gather(send_dy, 'expert', axis=0, tiled=True)  51.4 us
    reduce_scatter x1, waiting for transfers between devices, body(): lax.psum_scatter(d_part.astype(jnp.bfloat16), 'expert', scatter_dimension...  28.4 us
  transfers between devices with their start and end apart: 10, of which 7 were waited for; matrix products, arithmetic and copies ran while one was open for 2% of the time, Pallas kernels for 0%

profile of v1, /device:TPU:1, one launch (start us, length us, event | category | flops | bytes accessed | tf_op | source)
XLA Modules:
  0.0 865.0 jit_solution(10704545008492486408)
XLA Ops:
  7.2 0.0 copy-start
  7.2 0.0 all-gather.17.cloned.1.call-start
  7.2 0.7 all-gather.17.cloned.1.call-update
  7.9 0.0 all-gather.15.cloned.1.call-start
  8.0 0.7 all-gather.15.cloned.1.call-update
  8.7 0.0 all-gather.13.cloned.1.call-start
  8.7 0.7 all-gather.13.cloned.1.call-update
  9.4 0.0 reduce-scatter.2.cloned.1.call-start
  9.4 0.7 fusion.28
  10.1 0.1 select_reduce_fusion
  10.2 0.7 fusion.27
  10.9 0.2 convolution_convert_fusion.3
  11.1 54.4 %all_gather.23 = bf16[64,2048]{1,0:T(8,128)(2,1)S(1)} all-gather(bf16[8,2048]{1,0:T(8,128)(2,1)S(1)} %convolution_convert_fusion.3), channel_id=1, replica_groups=mesh['section'=8,'expert'=8,'dp'=8] {'expert'}, dimensions={0}, use_global_device_ids=true | all-gather | bytes 294912 | tf_op jit(solution)/shard_map/all_gather | solution.py:51
  65.5 1.3 convolution_convert_fusion.4
  66.8 51.4 %all_gather.21 = bf16[64,2048]{1,0:T(8,128)(2,1)S(1)} all-gather(bf16[8,2048]{1,0:T(8,128)(2,1)S(1)} %convolution_convert_fusion.4), channel_id=1, replica_groups=mesh['section'=8,'expert'=8,'dp'=8] {'expert'}, dimensions={0}, use_global_device_ids=true | all-gather | bytes 294912 | tf_op jit(solution)/shard_map/all_gather | solution.py:52
  118.2 85.7 %all-gather.17.cloned.1.call-done = bf16[1,2048,1024]{2,1,0:T(8,128)(2,1)} async-done(((bf16[1,2048,128]{2,1,0:T(8,128)(2,1)}), bf16[1,2048,1024]{2,1,0:T(8,128)(2,1)}) %all-gather.17.cloned.1.call-update) | async-done | bytes 4194320 | tf_op jit(solution)/shard_map/all_gather | solution.py:55
  203.9 3.0 fusion.2
  206.9 174.9 %all-gather.15.cloned.1.call-done = bf16[1,2048,1024]{2,1,0:T(8,128)(2,1)} async-done(((bf16[1,2048,128]{2,1,0:T(8,128)(2,1)}), bf16[1,2048,1024]{2,1,0:T(8,128)(2,1)}) %all-gather.15.cloned.1.call-update) | async-done | bytes 4194320 | tf_op jit(solution)/shard_map/all_gather | solution.py:56
  381.8 3.0 fusion.6
  384.9 175.2 %all-gather.13.cloned.1.call-done = bf16[1,2048,1024]{2,1,0:T(8,128)(2,1)} async-done(((bf16[1,2048,128]{2,1,0:T(8,128)(2,1)}), bf16[1,2048,1024]{2,1,0:T(8,128)(2,1)}) %all-gather.13.cloned.1.call-update) | async-done | bytes 4194320 | tf_op jit(solution)/shard_map/all_gather | solution.py:57
  560.0 3.3 fusion.23
  563.3 0.2 copy-done.2
  563.5 1.4 fusion
  564.9 2.1 fusion.17
  567.0 0.0 reduce-scatter.2.cloned.1.call-update
  567.0 0.0 all-gather.9.cloned.1.call-start
  567.1 0.5 all-gather.9.cloned.1.call-update
  567.6 0.0 all-gather.11.cloned.1.call-start
  567.6 0.5 all-gather.11.cloned.1.call-update
  568.2 0.7 copy_bitcast_fusion.2
  568.9 3.4 all-to-all-start
  572.3 0.7 copy_bitcast_fusion.1
  573.0 13.7 %all-to-all-done = bf16[64,8,128]{2,0,1:T(8,128)(2,1)S(1)} async-done(((bf16[64,8,128]{2,0,1:T(8,128)(2,1)}), bf16[64,8,128]{2,0,1:T(8,128)(2,1)S(1)}, u32[]{:S(2)}, u32[]{:S(2)}) %all-to-all-start) | async-done | bytes 131104 | tf_op jit(solution)/shard_map/all_to_all | solution.py:62
  586.7 3.4 all-to-all-start.1
  590.1 0.7 copy.22
  590.7 28.4 %reduce-scatter.2.cloned.1.call-done = bf16[8,2048]{1,0:T(8,128)(2,1)} async-done(((bf16[64,2048]{1,0:T(8,128)(2,1)}), bf16[8,2048]{1,0:T(8,128)(2,1)}) %reduce-scatter.2.cloned.1.call-update) | async-done | bytes 32784 | tf_op jit(solution)/shard_map/reduce_scatter | solution.py:60
  619.2 0.0 all-to-all-done.1
  619.2 7.4 all-to-all-start.2
  626.6 1.1 fusion.10
  627.7 4.8 collective-permute-start
  632.5 106.3 %all-gather.9.cloned.1.call-done = bf16[512,2048]{1,0:T(8,128)(2,1)} async-done(((bf16[64,2048]{1,0:T(8,128)(2,1)}), bf16[512,2048]{1,0:T(8,128)(2,1)}) %all-gather.9.cloned.1.call-update) | async-done | bytes 2097168 | tf_op jit(solution)/shard_map/all_gather | solution.py:67
  738.8 3.3 fusion.14
  742.1 1.6 fusion.15
  743.6 110.6 %all-gather.11.cloned.1.call-done = bf16[512,2048]{1,0:T(8,128)(2,1)} async-done(((bf16[64,2048]{1,0:T(8,128)(2,1)}), bf16[512,2048]{1,0:T(8,128)(2,1)}) %all-gather.11.cloned.1.call-update) | async-done | bytes 2097168 | tf_op jit(solution)/shard_map/all_gather | solution.py:68
  854.2 0.0 all-to-all-done.2
  854.2 3.1 fusion.16
  857.3 0.0 collective-permute-done
  857.4 0.8 copy.24
  (12 shorter events, 0.0 us)
Async XLA Ops:
  7.2 3.7 copy-start
  7.2 196.7 %all-gather.17.cloned.1.call-start = ((), (), s32[]{:S(2)}) async-start(), calls=%async_computation.9 | async-start | bytes 4718592 | tf_op jit(solution)/shard_map/all_gather | solution.py:55
  7.9 373.9 %all-gather.15.cloned.1.call-start = ((), (), s32[]{:S(2)}) async-start(), calls=%async_computation.8 | async-start | bytes 4718592 | tf_op jit(solution)/shard_map/all_gather | solution.py:56
  8.7 551.4 %all-gather.13.cloned.1.call-start = ((), (), s32[]{:S(2)}) async-start(), calls=%async_computation.7 | async-start | bytes 4718592 | tf_op jit(solution)/shard_map/all_gather | solution.py:57
  9.4 609.8 %reduce-scatter.2.cloned.1.call-start = ((), (), s32[]{:S(2)}) async-start(), calls=%async_computation.4 | async-start | bytes 294912 | tf_op jit(solution)/shard_map/reduce_scatter | solution.py:60
  65.5 319.4 %copy-start.4 = (bf16[64,2048]{1,0:T(8,128)(2,1)}, bf16[64,2048]{1,0:T(8,128)(2,1)S(1)}, u32[]{:S(2)}) copy-start(bf16[64,2048]{1,0:T(8,128)(2,1)S(1)} %all_gather.23) | copy-start | bytes 786436
  118.2 441.8 %copy-start.5 = (bf16[64,2048]{1,0:T(8,128)(2,1)}, bf16[64,2048]{1,0:T(8,128)(2,1)S(1)}, u32[]{:S(2)}) copy-start(bf16[64,2048]{1,0:T(8,128)(2,1)S(1)} %all_gather.21) | copy-start | bytes 786436
  560.0 3.4 copy-start.2
  560.0 4.8 copy-start.3
  564.9 61.7 %copy-start.6 = (bf16[1,128,2048]{2,1,0:T(8,128)(2,1)S(1)}, bf16[1,128,2048]{2,1,0:T(8,128)(2,1)}, u32[]{:S(2)}) copy-start(bf16[1,128,2048]{2,1,0:T(8,128)(2,1)} %param.7) | copy-start | bytes 1572868
  567.0 171.8 %all-gather.9.cloned.1.call-start = ((), (), s32[]{:S(2)}) async-start(), calls=%async_computation.5 | async-start | bytes 2359296 | tf_op jit(solution)/shard_map/all_gather | solution.py:67
  567.6 286.6 %all-gather.11.cloned.1.call-start = ((), (), s32[]{:S(2)}) async-start(), calls=%async_computation.6 | async-start | bytes 2359296 | tf_op jit(solution)/shard_map/all_gather | solution.py:68
  568.9 17.8 %all-to-all-start = ((bf16[64,8,128]{2,0,1:T(8,128)(2,1)}), bf16[64,8,128]{2,0,1:T(8,128)(2,1)S(1)}, u32[]{:S(2)}, u32[]{:S(2)}) async-start(bf16[64,8,128]{2,0,1:T(8,128)(2,1)} %copy_bitcast_fusion.2), calls=%async_computation.1 | async-start | bytes 262144 | tf_op jit(solution)/shard_map/all_to_all | solution.py:62
  586.7 32.5 %all-to-all-start.1 = ((bf16[64,8,128]{2,0,1:T(8,128)(2,1)}), bf16[64,8,128]{2,0,1:T(8,128)(2,1)S(1)}, u32[]{:S(2)}, u32[]{:S(2)}) async-start(bf16[64,8,128]{2,0,1:T(8,128)(2,1)} %copy_bitcast_fusion.1), calls=%async_computation.2 | async-start | bytes 262144 | tf_op jit(solution)/shard_map/all_to_all | solution.py:63
  619.2 235.0 %all-to-all-start.2 = ((bf16[64,8,128]{2,0,1:T(8,128)(2,1)}), bf16[64,8,128]{2,0,1:T(8,128)(2,1)S(1)}, u32[]{:S(2)}, u32[]{:S(2)}) async-start(bf16[64,8,128]{2,0,1:T(8,128)(2,1)} %bitcast.74), calls=%async_computation.3 | async-start | bytes 262144 | tf_op jit(solution)/shard_map/all_to_all | solution.py:64
  627.7 229.6 %collective-permute-start = (bf16[128,2048]{1,0:T(8,128)(2,1)S(1)}, bf16[128,2048]{1,0:T(8,128)(2,1)S(1)}, u32[]{:S(2)}, u32[]{:S(2)}) collective-permute-start(bf16[128,2048]{1,0:T(8,128)(2,1)S(1)} %fusion.10), channel_id=1, source_target_pairs={{0,448},{64,0},{128,64},{192,128},{256,192},{320,256},{384,320},{4... | collective-permute-start | bytes 1572872 | tf_op jit(solution)/shard_map/ppermute | solution.py:12
  738.8 3.3 copy-start.1
Sparse Core Ops, SparseCore 0:
  11.1 192.7 all-gather.16
  207.0 174.8 all-gather.14
  384.9 175.0 all-gather.12
  567.1 52.0 reduce-scatter.1
  623.3 115.4 all-gather.8
  742.9 111.2 all-gather.10

commit v2 on v1

v2 whole, which is shorter than its diff:
```python
import jax
import jax.numpy as jnp
from jax import lax
from jax.sharding import PartitionSpec as P

SLOT = 8
GROUP = ("expert", "dp")


def shifted(value, axis, steps):
    count = lax.axis_size(axis)
    pairs = [(source, (source + steps) % count) for source in range(count)]
    return lax.ppermute(value, axis, pairs)


def body(layer_input, output_grad, expert_ids, w_gate, w_up, w_down):
    inputs = layer_input[0]
    grads = output_grad[0]
    routes = expert_ids[0]
    chosen = (routes == 0).astype(jnp.int32)
    order = jnp.arange(chosen.shape[0], dtype=jnp.int32)
    within = jnp.sum(jnp.where(order[None, :] < order[:, None], chosen[None, :], 0), axis=1)
    target = jnp.where(chosen > 0, within, SLOT)
    places = jnp.arange(SLOT, dtype=jnp.int32)
    match = (target[None, :] == places[:, None]).astype(jnp.bfloat16)
    send_x = jnp.dot(match, inputs, preferred_element_type=jnp.float32).astype(jnp.bfloat16)
    send_dy = jnp.dot(match, grads, preferred_element_type=jnp.float32).astype(jnp.bfloat16)
    moved_grads = shifted(grads, "section", -1)
    moved_match = shifted(match, "section", -1)
    rows = lax.all_gather(jnp.stack([send_x, send_dy]), GROUP, axis=1, tiled=True)
    x_rows, dy_rows = rows[0], rows[1]
    w_both = jnp.concatenate([w_gate[0], w_up[0]], axis=1)
    both = jnp.dot(x_rows, w_both, preferred_element_type=jnp.float32)
    width = w_gate.shape[2]
    gate, upper = both[:, :width], both[:, width:]
    sigma = jax.nn.sigmoid(gate)
    active = gate * sigma
    hidden = (active * upper).astype(jnp.bfloat16)
    d_hidden = jnp.dot(dy_rows, w_down[0], preferred_element_type=jnp.float32)
    d_gate = (d_hidden * upper * sigma * (1.0 + gate * (1.0 - sigma))).astype(jnp.bfloat16)
    d_up = (d_hidden * active).astype(jnp.bfloat16)
    d_both = jnp.concatenate([d_gate, d_up], axis=1)
    back_dims = (((1,), (1,)), ((), ()))
    d_part = lax.dot_general(d_both, w_both, back_dims, preferred_element_type=jnp.float32)
    d_rows = lax.psum_scatter(d_part.astype(jnp.bfloat16), GROUP, scatter_dimension=0, tiled=True)
    d_rows = shifted(d_rows, "section", -1)
    row_dims = (((0,), (0,)), ((), ()))
    part_both = lax.dot_general(x_rows, d_both, row_dims, preferred_element_type=jnp.float32).astype(jnp.bfloat16)
    part_down = lax.dot_general(dy_rows, hidden, row_dims, preferred_element_type=jnp.float32).astype(jnp.bfloat16)
    term = lax.dot_general(
        moved_match, d_rows, (((0,), (0,)), ((), ())), preferred_element_type=jnp.float32
    )
    token_grad = (moved_grads.astype(jnp.float32) + term).astype(jnp.bfloat16)
    return (token_grad[None], part_both[None, :, :width], part_both[None, :, width:], part_down[None])


def solution(mesh):
    rows = P("section", ("expert", "dp"), None)
    weights = P("section", None, ("expert", "dp"))
    in_specs = (rows, rows, P("section", ("expert", "dp")), weights, weights, weights)
    out_specs = (rows, weights, weights, weights)
    return jax.shard_map(body, mesh=mesh, in_specs=in_specs, out_specs=out_specs, check_vma=False)
```

time: 866 us -> 1200 us (1.39)
  waiting for transfers between devices: 698 us -> 1050 us
  blocking collectives: 106 us -> 0 us
  starting transfers between devices: 19.3 us -> 116 us
    reduce_scatter x1, waiting for transfers between devices: 28.4 us -> 473 us  [body(): lax.psum_scatter(d_part.astype(jnp.bfloat16), GROUP, scatter_dimension=0,...]
    ppermute x1 -> x3, starting transfers between devices: 4.78 us -> 116 us  [shifted(): return lax.ppermute(value, axis, pairs)]
    all_gather x2 -> x0, blocking collectives: 106 us -> none  [the longest x1 54.4 us: body(): lax.all_gather(send_x, 'expert', axis=0, tiled=True)]
    all_gather x5 -> x1, waiting for transfers between devices: 653 us -> 578 us  [body(): lax.all_gather(jnp.stack([send_x, send_dy]), GROUP, axis=1, tiled=True)]
    all_to_all x3 -> x0, starting transfers between devices: 14.2 us -> none  [the longest x1 7.42 us: body(): lax.all_to_all(hidden, 'dp', split_axis=1, concat_axis=0, tiled=True)]
    all_to_all x3 -> x0, waiting for transfers between devices: 13.7 us -> none  [the longest x1 13.7 us: body(): lax.all_to_all(d_gate, 'dp', split_axis=1, concat_axis=0, tiled=True)]
  transfers between devices with their start and end apart: 10 -> 5, of which waited for: 7 -> 2; matrix products, arithmetic and copies ran while one was open for 2% -> 1% of each run, Pallas kernels for 0% -> 0%
where the time goes in v2:
time: 1200 us
  waiting for transfers between devices  1050 us (88%)
  starting transfers between devices  116 us (10%)
  matrix products  14.8 us (1%)
  between operations  14.1 us (1%)
    all_gather x1, waiting for transfers between devices, body(): lax.all_gather(jnp.stack([send_x, send_dy]), GROUP, axis=1, tiled=True)  578 us
    reduce_scatter x1, waiting for transfers between devices, body(): lax.psum_scatter(d_part.astype(jnp.bfloat16), GROUP, scatter_dimension=0,...  473 us
    ppermute x3, starting transfers between devices, shifted(): return lax.ppermute(value, axis, pairs)  116 us
  transfers between devices with their start and end apart: 5, of which 2 were waited for; matrix products, arithmetic and copies ran while one was open for 1% of the time, Pallas kernels for 0%

profile of v2, /device:TPU:1, one launch (start us, length us, event | category | flops | bytes accessed | tf_op | source)
XLA Modules:
  0.0 1200.4 jit_solution(17072513962563415594)
XLA Ops:
  7.2 0.0 copy-start
  7.2 0.0 all-gather.2.cloned.1.call-start
  7.2 0.7 fusion.14
  7.9 0.1 select_reduce_fusion
  8.0 0.7 fusion.13
  8.7 1.2 fusion.2
  9.9 1.2 fusion.1
  11.2 0.6 pad_maximum_fusion.6
  11.8 0.0 all-gather.2.cloned.1.call-update
  11.8 0.0 reduce-scatter.2.cloned.1.call-start
  11.9 577.8 %all-gather.2.cloned.1.call-done = bf16[2,512,2048]{2,1,0:T(8,128)(2,1)} async-done(((bf16[2,8,2048]{2,1,0:T(8,128)(2,1)}), bf16[2,512,2048]{2,1,0:T(8,128)(2,1)}) %all-gather.2.cloned.1.call-update) | async-done | bytes 4194320 | tf_op jit(solution)/shard_map/all_gather | solution.py:30
  589.6 0.0 copy-start.4
  589.6 2.7 fusion.4
  592.4 0.0 copy-done
  592.4 0.4 copy-done.4
  592.8 0.0 copy-start.1
  592.8 0.0 copy-start.2
  592.8 0.9 multiply_convert_fusion.2
  593.6 0.2 copy-done.1
  593.8 0.2 copy-done.2
  594.0 2.1 convolution_convert_fusion
  596.1 0.0 copy-start.3
  596.1 0.0 reduce-scatter.2.cloned.1.call-update
  596.1 58.9 %collective-permute-start.1 = (bf16[8,128]{1,0:T(8,128)(2,1)S(1)}, bf16[8,128]{1,0:T(8,128)(2,1)S(1)}, u32[]{:S(2)}, u32[]{:S(2)}) collective-permute-start(bf16[8,128]{1,0:T(8,128)(2,1)S(1)} %fusion.10), channel_id=1, source_target_pairs={{0,448},{64,0},{128,64},{192,128},{256,192},{320,256},{384,320},{4... | collective-permute-start | bytes 6152 | tf_op jit(solution)/shard_map/ppermute | solution.py:13
  655.0 0.0 copy-done.3
  655.0 1.0 collective-permute-start
  656.0 2.4 convolution_convert_fusion.1
  658.4 1.0 slice_bitcast_fusion.6
  659.4 473.4 %reduce-scatter.2.cloned.1.call-done = bf16[8,2048]{1,0:T(8,128)(2,1)} async-done(((bf16[512,2048]{1,0:T(8,128)(2,1)}), bf16[8,2048]{1,0:T(8,128)(2,1)}) %reduce-scatter.2.cloned.1.call-update) | async-done | bytes 32784 | tf_op jit(solution)/shard_map/reduce_scatter | solution.py:45
  1132.8 56.4 %collective-permute-start.2 = (bf16[8,2048]{1,0:T(8,128)(2,1)}, bf16[8,2048]{1,0:T(8,128)(2,1)S(1)}, u32[]{:S(2)}, u32[]{:S(2)}) collective-permute-start(bf16[8,2048]{1,0:T(8,128)(2,1)} %reduce-scatter.2.cloned.1.call-done), channel_id=1, source_target_pairs={{0,448},{64,0},{128,64},{192,128},{256,192},{320,256},{384,320},{4... | collective-permute-start | bytes 98312 | tf_op jit(solution)/shard_map/ppermute | solution.py:13
  1189.2 3.2 fusion
  1192.4 0.0 collective-permute-done.1
  1192.4 0.0 collective-permute-done
  1192.4 0.0 collective-permute-done.2
  1192.4 1.1 fusion.5
  (1 shorter events, 0.0 us)
Async XLA Ops:
  7.2 585.2 %copy-start = (bf16[1,2048,128]{2,1,0:T(8,128)(2,1)S(1)}, bf16[1,2048,128]{2,1,0:T(8,128)(2,1)}, u32[]{:S(2)}) copy-start(bf16[1,2048,128]{2,1,0:T(8,128)(2,1)} %param.11) | copy-start | bytes 1572868
  7.2 582.5 %all-gather.2.cloned.1.call-start = ((), (), s32[]{:S(2)}) async-start(), calls=%async_computation.1 | async-start | bytes 4259840 | tf_op jit(solution)/shard_map/all_gather | solution.py:30
  11.8 1121.0 %reduce-scatter.2.cloned.1.call-start = ((), (), s32[]{:S(2)}) async-start(), calls=%async_computation.2 | async-start | bytes 2129920 | tf_op jit(solution)/shard_map/reduce_scatter | solution.py:45
  589.6 3.1 copy-start.4
  592.8 1.0 copy-start.1
  592.8 1.2 copy-start.2
  596.1 58.9 %copy-start.3 = (bf16[1,128,2048]{2,1,0:T(8,128)(2,1)S(1)}, bf16[1,128,2048]{2,1,0:T(8,128)(2,1)}, u32[]{:S(2)}) copy-start(bf16[1,128,2048]{2,1,0:T(8,128)(2,1)} %param.7) | copy-start | bytes 1572868
  596.1 596.3 %collective-permute-start.1 = (bf16[8,128]{1,0:T(8,128)(2,1)S(1)}, bf16[8,128]{1,0:T(8,128)(2,1)S(1)}, u32[]{:S(2)}, u32[]{:S(2)}) collective-permute-start(bf16[8,128]{1,0:T(8,128)(2,1)S(1)} %fusion.10), channel_id=1, source_target_pairs={{0,448},{64,0},{128,64},{192,128},{256,192},{320,256},{384,320},{4... | collective-permute-start | bytes 6152 | tf_op jit(solution)/shard_map/ppermute | solution.py:13
  655.0 537.4 %collective-permute-start = (bf16[128,2048]{1,0:T(8,128)(2,1)S(1)}, bf16[128,2048]{1,0:T(8,128)(2,1)S(1)}, u32[]{:S(2)}, u32[]{:S(2)}) collective-permute-start(bf16[128,2048]{1,0:T(8,128)(2,1)S(1)} %bitcast.47), channel_id=1, source_target_pairs={{0,448},{64,0},{128,64},{192,128},{256,192},{320,256},{384,320},{4... | collective-permute-start | bytes 1572872 | tf_op jit(solution)/shard_map/ppermute | solution.py:13
  1132.8 59.6 %collective-permute-start.2 = (bf16[8,2048]{1,0:T(8,128)(2,1)}, bf16[8,2048]{1,0:T(8,128)(2,1)S(1)}, u32[]{:S(2)}, u32[]{:S(2)}) collective-permute-start(bf16[8,2048]{1,0:T(8,128)(2,1)} %reduce-scatter.2.cloned.1.call-done), channel_id=1, source_target_pairs={{0,448},{64,0},{128,64},{192,128},{256,192},{320,256},{384,320},{4... | collective-permute-start | bytes 98312 | tf_op jit(solution)/shard_map/ppermute | solution.py:13
Sparse Core Ops, SparseCore 0:
  11.9 577.6 all-gather.1
  596.2 536.5 reduce-scatter.1

commit v3 on v2

v3 whole, which is shorter than its diff:
```python
import functools

import jax
import jax.numpy as jnp
from jax import lax
from jax.experimental import pallas as pl
from jax.experimental.pallas import tpu as pltpu
from jax.sharding import PartitionSpec as P

SLOT = 8
Z_HI = 2
F32 = jnp.float32
BF16 = jnp.bfloat16
ROWS_DIM = (((0,), (0,)), ((), ()))
BACK_DIM = (((1,), (1,)), ((), ()))


def slot_match(ids):
    tokens = ids.shape[1]
    chosen = jnp.broadcast_to((ids == 0).astype(F32), (SLOT, tokens))
    before = lax.broadcasted_iota(jnp.int32, (tokens, tokens), 0)
    after = lax.broadcasted_iota(jnp.int32, (tokens, tokens), 1)
    order = (before < after).astype(F32).astype(BF16)
    within = jnp.dot(chosen.astype(BF16), order, preferred_element_type=F32)
    place = lax.broadcasted_iota(jnp.int32, (SLOT, tokens), 0).astype(F32)
    return jnp.where(within == place, chosen, 0.0).astype(BF16)


def kernel(cfg, ids_ref, x_ref, dy_ref, wg_ref, wu_ref, wd_ref, og_ref, gg_ref, gu_ref, gd_ref,
           x_v, dy_v, w_gu, w_dn, shift_dy, shift_ids, g_a, g_b, x_all, dy_all, d_gu, hid, p_a, p_b,
           sa_r, ra_r, sa_l, ra_l, sy_b, ry_b, sum_b, sb_r, rb_r, sb_l, rb_l, sy_a, ry_a, fin_a, fin_b, got_a, got_b,
           og_v, gg_v, gu_v, gd_v,
           loc, sh_s, sh_r, a1_s, a1_r, ar_s, ar_r, al_s, al_r, br_s, br_r, bl_s, bl_r, by_s, by_r,
           rar_s, rar_r, ral_s, ral_r, rby_s, rby_r, rbr_s, rbr_r, rbl_s, rbl_r, ray_s, ray_r):
    Y, Z, D, CA, RA = cfg
    HA, HB = RA // 2, (D - RA) // 2
    K = Z // 2
    n_sec, n_exp = lax.axis_size("section"), lax.axis_size("expert")
    sec, ex, dp = lax.axis_index("section"), lax.axis_index("expert"), lax.axis_index("dp")
    y, z = dp // Z_HI, lax.rem(dp, Z_HI) * n_exp + ex

    def wrap(v, n):
        return lax.rem(v + n, n)

    def at(yy, zz):
        return {"expert": lax.rem(zz, n_exp), "dp": yy * Z_HI + zz // n_exp}

    z_right, z_left = at(y, wrap(z + 1, Z)), at(y, wrap(z - 1, Z))
    y_right, y_left = at(wrap(y + 1, Y), z), at(wrap(y - 1, Y), z)
    y_far = at(wrap(y + 2, Y), z)
    s_prev, s_next = {"section": wrap(sec - 1, n_sec)}, {"section": wrap(sec + 1, n_sec)}

    def remote(src, dst, s_sem, r_sem, to):
        return pltpu.make_async_remote_copy(
            src_ref=src, dst_ref=dst, send_sem=s_sem, recv_sem=r_sem, device_id=to, device_id_type=pl.DeviceIdType.MESH)

    barrier = pltpu.get_barrier_semaphore()
    partners = (z_right, z_left, y_right, y_left, y_far, s_prev, s_next)
    for to in partners:
        pl.semaphore_signal(barrier, inc=1, device_id=to, device_id_type=pl.DeviceIdType.MESH)

    half = w_gu.shape[1] // 2
    loads = [
        pltpu.make_async_copy(x_ref, x_v, loc.at[0]),
        pltpu.make_async_copy(dy_ref, dy_v, loc.at[1]),
        pltpu.make_async_copy(wg_ref, w_gu.at[:, pl.ds(0, half)], loc.at[2]),
        pltpu.make_async_copy(wu_ref, w_gu.at[:, pl.ds(half, half)], loc.at[3]),
        pltpu.make_async_copy(wd_ref, w_dn, loc.at[4]),
    ]
    for copy in loads:
        copy.start()
    match = slot_match(ids_ref[...])
    loads[0].wait()
    loads[1].wait()
    own = jnp.concatenate([
        jnp.dot(match, x_v[...], preferred_element_type=F32),
        jnp.dot(match, dy_v[...], preferred_element_type=F32)], axis=0).astype(BF16)
    g_a[z, y] = own[:, :CA]
    g_b[z, y] = own[:, CA:]
    pl.semaphore_wait(barrier, len(partners))

    def a1(j, to):
        return remote(g_a.at[z, y], g_a.at[z, y], a1_s.at[j], a1_r.at[j], to)

    def a1_in(j, yy):
        return remote(g_a.at[z, yy], g_a.at[z, yy], a1_s.at[j], a1_r.at[j], y_right)

    def a_right(k, block):
        return remote(g_a.at[block], g_a.at[block], ar_s.at[k], ar_r.at[k], z_right)

    def a_left(k, block):
        return remote(g_a.at[block], g_a.at[block], al_s.at[k], al_r.at[k], z_left)

    def b_right(k, block):
        return remote(g_b.at[block, y], g_b.at[block, y], br_s.at[k], br_r.at[k], z_right)

    def b_left(k, block):
        return remote(g_b.at[block, y], g_b.at[block, y], bl_s.at[k], bl_r.at[k], z_left)

    def b_y(kind, o, yy, to):
        block = wrap(z - o, Z)
        return remote(g_b.at[block, yy], g_b.at[block, yy], by_s.at[kind, o], by_r.at[kind, o], to)

    def spread(o):
        b_y(0, o, y, y_right).start()
        b_y(1, o, y, y_left).start()

    for j, to in enumerate((y_right, y_left, y_far)):
        a1(j, to).start()
    b_right(0, z).start()
    b_left(0, z).start()
    spread(0)
    shift = [remote(ids_ref, shift_ids, sh_s.at[0], sh_r.at[0], s_prev), remote(dy_ref, shift_dy, sh_s.at[1], sh_r.at[1], s_prev)]
    for copy in shift:
        copy.start()
    for j, step in enumerate((-1, 1, 2)):
        a1_in(j, wrap(y + step, Y)).wait_recv()
    a_right(0, z).start()
    a_left(0, z).start()

    def pass_right(o):
        b_y(0, o, wrap(y - 1, Y), y_right).wait_recv()
        b_y(2, o, wrap(y - 1, Y), y_right).start()

    def pass_left(o):
        b_y(1, o, wrap(y + 1, Y), y_left).wait_recv()
        b_y(2, o, wrap(y + 1, Y), y_left).start()

    def gather_step(k, _):
        zr, zl = wrap(z - k, Z), wrap(z + k, Z)

        @pl.when(k < K)
        def _():
            b_right(k - 1, zr).wait_recv()

            @pl.when(k < K - 1)
            def _():
                b_right(k, zr).start()

            spread(k)

        b_left(k - 1, zl).wait_recv()

        @pl.when(k < K)
        def _():
            b_left(k, zl).start()

        spread(Z - k)
        a_right(k - 1, zr).wait_recv()

        @pl.when(k < K)
        def _():
            a_right(k, zr).start()
            a_left(k - 1, zl).wait_recv()

            @pl.when(k < K - 1)
            def _():
                a_left(k, zl).start()

        pass_right(k - 1)

        @pl.when(k > 1)
        def _():
            pass_left(Z - k + 1)

        return 0

    lax.fori_loop(1, K + 1, gather_step, 0)
    pass_left(K)

    def gather_end(o, _):
        @pl.when(o < K)
        def _():
            b_y(1, o, wrap(y + 1, Y), y_left).wait_recv()

        @pl.when(o >= K)
        def _():
            b_y(0, o, wrap(y - 1, Y), y_right).wait_recv()

        b_y(2, o, wrap(y + 2, Y), y_right).wait_recv()
        return 0

    lax.fori_loop(0, Z, gather_end, 0)
    for copy in loads[2:]:
        copy.wait()

    CZ = 128 // (Y * SLOT)

    def unpack(c, _):
        rows = pl.ds(pl.multiple_of(c * (Y * SLOT), Y * SLOT), Y * SLOT)
        for ref, lo, hi in ((g_a, 0, CA), (g_b, CA, D)):
            both = ref[c].astype(F32)
            x_all[rows, lo:hi] = both[:, :SLOT].reshape(Y * SLOT, hi - lo).astype(BF16)
            dy_all[rows, lo:hi] = both[:, SLOT:].reshape(Y * SLOT, hi - lo).astype(BF16)
        return 0

    lax.fori_loop(0, Z, unpack, 0)

    def forward(c, _):
        rows = pl.ds(pl.multiple_of(c * 128, 128), 128)
        both = jnp.dot(x_all[rows, :], w_gu[...], preferred_element_type=F32)
        d_hidden = jnp.dot(dy_all[rows, :], w_dn[...], preferred_element_type=F32)
        gate, upper = both[:, :half], both[:, half:]
        sigma = jax.nn.sigmoid(gate)
        active = gate * sigma
        hid[rows, :] = (active * upper).astype(BF16)
        d_gu[rows, :half] = (d_hidden * upper * sigma * (1.0 + gate * (1.0 - sigma))).astype(BF16)
        d_gu[rows, half:] = (d_hidden * active).astype(BF16)
        CW = 256
        for lo in range(0, D, CW):
            part = lax.dot_general(d_gu[rows, :], w_gu[lo:lo + CW, :], BACK_DIM, preferred_element_type=F32)
            if lo < RA:
                p_a[pl.ds(c * CZ, CZ), :, lo:lo + CW] = part.reshape(CZ, Y * SLOT, CW)
            else:
                cut = part.reshape(CZ, Y, SLOT, CW)
                for yy in range(Y):
                    p_b[yy, pl.ds(c * CZ, CZ), :, lo - RA:lo - RA + CW] = cut[:, yy]
        return 0

    lax.fori_loop(0, Z // CZ, forward, 0)

    def ra_right(k):
        return remote(sa_r.at[k], ra_r.at[k], rar_s.at[k], rar_r.at[k], z_right)

    def ra_left(k):
        return remote(sa_l.at[k], ra_l.at[k], ral_s.at[k], ral_r.at[k], z_left)

    def rb_right(k):
        return remote(sb_r.at[k], rb_r.at[k], rbr_s.at[k], rbr_r.at[k], z_right)

    def rb_left(k):
        return remote(sb_l.at[k], rb_l.at[k], rbl_s.at[k], rbl_r.at[k], z_left)

    def rb_y(j):
        return remote(sy_b.at[j], ry_b.at[j], rby_s.at[j], rby_r.at[j], y_right if j % 2 == 0 else y_left)

    def ra_y(j, to):
        return remote(sy_a.at[j], ry_a.at[j], ray_s.at[j], ray_r.at[j], to)

    def ring_a(k):
        if k < K:
            value = p_a[wrap(z + K - k, Z)]
            if k > 0:
                ra_right(k - 1).wait_recv()
                value = value + ra_r[k - 1].astype(F32)
            sa_r[k] = value.astype(BF16)
            ra_right(k).start()
        if k < K - 1:
            value = p_a[wrap(z - K + 1 + k, Z)]
            if k > 0:
                ra_left(k - 1).wait_recv()
                value = value + ra_l[k - 1].astype(F32)
            sa_l[k] = value.astype(BF16)
            ra_left(k).start()

    def ring_b(k):
        if k < K - 1:
            value = sum_b[wrap(z + K - 1 - k, Z)]
            if k > 0:
                rb_right(k - 1).wait_recv()
                value = value + rb_r[k - 1].astype(F32)
            sb_r[k] = value.astype(BF16)
            rb_right(k).start()
        if k < K:
            value = sum_b[wrap(z - K + k, Z)]
            if k > 0:
                rb_left(k - 1).wait_recv()
                value = value + rb_l[k - 1].astype(F32)
            sb_l[k] = value.astype(BF16)
            rb_left(k).start()

    def flat(yy, lo):
        return p_b[yy, :, :, lo:lo + HB].reshape(Z * SLOT, HB)

    def y_first():
        far, nxt, prv = wrap(y + 2, Y), wrap(y + 1, Y), wrap(y - 1, Y)
        for j, value in enumerate((flat(far, 0), flat(far, HB), flat(nxt, HB), flat(prv, 0))):
            sy_b[j] = value.astype(BF16)
            rb_y(j).start()

    def y_second():
        nxt, prv = wrap(y + 1, Y), wrap(y - 1, Y)
        rb_y(0).wait_recv()
        sy_b[4] = (flat(nxt, 0) + ry_b[0].astype(F32)).astype(BF16)
        rb_y(4).start()
        rb_y(1).wait_recv()
        sy_b[5] = (flat(prv, HB) + ry_b[1].astype(F32)).astype(BF16)
        rb_y(5).start()

    def y_sum():
        for j in range(2, 6):
            rb_y(j).wait_recv()
        first = flat(y, 0) + ry_b[4].astype(F32) + ry_b[3].astype(F32)
        second = flat(y, HB) + ry_b[2].astype(F32) + ry_b[5].astype(F32)
        sum_b[:, :SLOT, :] = first.reshape(Z, SLOT, HB)
        sum_b[:, SLOT:, :] = second.reshape(Z, SLOT, HB)

    steps = 8
    WD = D // steps

    def weights(j):
        cols = slice(j * WD, (j + 1) * WD)
        part = lax.dot_general(x_all[:, cols], d_gu[...], ROWS_DIM, preferred_element_type=F32).astype(BF16)
        gg_v[cols, :] = part[:, :half]
        gu_v[cols, :] = part[:, half:]
        gd_v[cols, :] = lax.dot_general(dy_all[:, cols], hid[...], ROWS_DIM, preferred_element_type=F32).astype(BF16)

    todo = list(range(steps))

    def some_weights():
        if todo:
            weights(todo.pop(0))

    ring_a(0)
    y_first()
    some_weights()
    ring_a(1)
    y_second()
    some_weights()
    ring_a(2)
    some_weights()
    ring_a(3) if K > 3 else None
    y_sum()
    ring_b(0)
    some_weights()
    done_a, done_b = min(4, K), 1
    while done_a < K:
        ring_a(done_a)
        ring_b(done_b)
        done_a, done_b = done_a + 1, done_b + 1
        some_weights()
    while todo:
        some_weights()
    outs = [
        pltpu.make_async_copy(gg_v, gg_ref, loc.at[0]),
        pltpu.make_async_copy(gu_v, gu_ref, loc.at[1]),
        pltpu.make_async_copy(gd_v, gd_ref, loc.at[2]),
    ]
    for copy in outs:
        copy.start()
    ra_right(K - 1).wait_recv()
    ra_left(K - 2).wait_recv()
    total = p_a[z] + ra_r[K - 1].astype(F32) + ra_l[K - 2].astype(F32)
    total = total.reshape(Y, SLOT, RA)
    p_y = jnp.concatenate([total[:, :, :HA], total[:, :, HA:]], axis=1)
    fin_y = p_y.astype(BF16)
    for yy in range(Y):
        sy_a[3 + yy] = fin_y[yy]
    y_peers = ((wrap(y + 1, Y), y_right), (wrap(y - 1, Y), y_left), (wrap(y + 2, Y), y_far))
    for j, (yy, to) in enumerate(y_peers):
        sy_a[j] = sy_a[3 + yy]
        ra_y(j, to).start()
    while done_b < K:
        ring_b(done_b)
        done_b += 1
    for j in range(3):
        ra_y(j, y_right).wait_recv()
    value = sy_a[3 + y].astype(F32)
    for j in range(3):
        value = value + ry_a[j].astype(F32)
    fin_a[...] = value.astype(BF16)
    back = [remote(fin_a, got_a, sh_s.at[2], sh_r.at[2], s_prev), remote(fin_b, got_b, sh_s.at[3], sh_r.at[3], s_prev)]
    back[0].start()
    rb_right(K - 2).wait_recv()
    rb_left(K - 1).wait_recv()
    fin_b[...] = (sum_b[z] + rb_r[K - 2].astype(F32) + rb_l[K - 1].astype(F32)).astype(BF16)
    back[1].start()

    for copy in shift:
        copy.wait_recv()
    match = slot_match(shift_ids[...])
    back[0].wait_recv()

    def finish(got, base, width):
        rows = got.astype(F32)
        for j in range(2):
            lo = base + j * width
            piece = rows[j * SLOT:(j + 1) * SLOT].astype(BF16)
            term = lax.dot_general(match, piece, ROWS_DIM, preferred_element_type=F32)
            og_v[:, lo:lo + width] = (shift_dy[:, lo:lo + width].astype(F32) + term).astype(BF16)

    finish(got_a[...], 0, HA)
    back[1].wait_recv()
    finish(got_b[...], RA, HB)
    last = pltpu.make_async_copy(og_v, og_ref, loc.at[3])
    last.start()

    for copy in shift + back:
        copy.wait_send()
    for j, to in enumerate((y_right, y_left, y_far)):
        a1(j, to).wait_send()
        ra_y(j, to).wait_send()
    for j in range(6):
        rb_y(j).wait_send()
    for k in range(K):
        a_right(k, z).wait_send()
        b_left(k, z).wait_send()
        ra_right(k).wait_send()
        rb_left(k).wait_send()
        if k < K - 1:
            a_left(k, z).wait_send()
            b_right(k, z).wait_send()
            ra_left(k).wait_send()
            rb_right(k).wait_send()

    def sent(o, _):
        for kind in range(3):
            b_y(kind, o, y, y_right).wait_send()
        return 0

    lax.fori_loop(0, Z, sent, 0)
    for copy in outs + [last]:
        copy.wait()


def split(width):
    unit = 256
    return max(unit, (width * 3 // 8) // unit * unit)


def body(Z_AXIS, layer_input, output_grad, expert_ids, w_gate, w_up, w_down):
    Y, Z = Z_AXIS
    _, tokens, D = layer_input.shape
    hidden = w_gate.shape[2]
    CA = RA = split(D)
    K = Z // 2
    rows = Y * Z * SLOT
    CB, RB = D - CA, D - RA
    V, DMA = pltpu.VMEM, pltpu.SemaphoreType.DMA
    scratch = [
        V((tokens, D), BF16), V((tokens, D), BF16), V((D, 2 * hidden), BF16), V((D, hidden), BF16),
        V((tokens, D), BF16), V((1, tokens), jnp.int32),
        V((Z, Y, 2 * SLOT, CA), BF16), V((Z, Y, 2 * SLOT, CB), BF16),
        V((rows, D), BF16), V((rows, D), BF16), V((rows, 2 * hidden), BF16), V((rows, hidden), BF16),
        V((Z, Y * SLOT, RA), F32), V((Y, Z, SLOT, RB), F32),
        V((K, Y * SLOT, RA), BF16), V((K, Y * SLOT, RA), BF16), V((K - 1, Y * SLOT, RA), BF16), V((K - 1, Y * SLOT, RA), BF16),
        V((6, Z * SLOT, RB // 2), BF16), V((6, Z * SLOT, RB // 2), BF16), V((Z, 2 * SLOT, RB // 2), F32),
        V((K - 1, 2 * SLOT, RB // 2), BF16), V((K - 1, 2 * SLOT, RB // 2), BF16),
        V((K, 2 * SLOT, RB // 2), BF16), V((K, 2 * SLOT, RB // 2), BF16),
        V((3 + Y, 2 * SLOT, RA // 2), BF16), V((3, 2 * SLOT, RA // 2), BF16),
        V((2 * SLOT, RA // 2), BF16), V((2 * SLOT, RB // 2), BF16), V((2 * SLOT, RA // 2), BF16), V((2 * SLOT, RB // 2), BF16),
        V((tokens, D), BF16), V((D, hidden), BF16), V((D, hidden), BF16), V((D, hidden), BF16),
        DMA((5,)), DMA((4,)), DMA((4,)), DMA((3,)), DMA((3,)),
        DMA((K,)), DMA((K,)), DMA((K,)), DMA((K,)), DMA((K,)), DMA((K,)), DMA((K,)), DMA((K,)),
        DMA((3, Z)), DMA((3, Z)),
        DMA((K,)), DMA((K,)), DMA((K,)), DMA((K,)), DMA((6,)), DMA((6,)),
        DMA((K,)), DMA((K,)), DMA((K,)), DMA((K,)), DMA((3,)), DMA((3,)),
    ]
    anywhere = pl.BlockSpec(memory_space=pl.ANY)
    weight = jax.ShapeDtypeStruct((D, hidden), BF16)
    token_grad, grad_gate, grad_up, grad_down = pl.pallas_call(
        functools.partial(kernel, (Y, Z, D, CA, RA)),
        out_shape=(jax.ShapeDtypeStruct((tokens, D), BF16), weight, weight, weight),
        in_specs=[pl.BlockSpec(memory_space=pltpu.VMEM)] + [anywhere] * 5,
        out_specs=(anywhere,) * 4,
        scratch_shapes=scratch,
        compiler_params=pltpu.CompilerParams(collective_id=0, has_side_effects=True, vmem_limit_bytes=56 << 20),
    )(expert_ids, layer_input[0], output_grad[0], w_gate[0], w_up[0], w_down[0])
    return token_grad[None], grad_gate[None], grad_up[None], grad_down[None]


def solution(mesh):
    rows = P("section", ("expert", "dp"), None)
    weights = P("section", None, ("expert", "dp"))
    in_specs = (rows, rows, P("section", ("expert", "dp")), weights, weights, weights)
    out_specs = (rows, weights, weights, weights)
    size = (mesh.shape["dp"] // Z_HI, mesh.shape["expert"] * Z_HI)
    return jax.shard_map(functools.partial(body, size), mesh=mesh, in_specs=in_specs, out_specs=out_specs, check_vma=False)
```

time: 1200 us -> 108 us (0.09)
  waiting for transfers between devices: 1050 us -> 0 us
  starting transfers between devices: 116 us -> 0 us
  Pallas kernels: 0 us -> 102 us
  matrix products: 14.8 us -> 0 us
  between operations: 14.1 us -> 0.65 us
    all_gather x1 -> x0, waiting for transfers between devices: 578 us -> none  [body(): lax.all_gather(jnp.stack([send_x, send_dy]), GROUP, axis=1, tiled=True)]
    reduce_scatter x1 -> x0, waiting for transfers between devices: 473 us -> none  [body(): lax.psum_scatter(d_part.astype(jnp.bfloat16), GROUP, scatter_dimension=0,...]
    ppermute x3 -> x0, starting transfers between devices: 116 us -> none  [shifted(): return lax.ppermute(value, axis, pairs)]
    pallas_call x0 -> x1, Pallas kernels: none -> 102 us  [body(): pl.pallas_call(functools.partial(kernel, (Y, Z, D, CA, RA)), out_shape=(j...]
    dot_general x8 -> x0, matrix products: 14.8 us -> none  [the longest x1 3.18 us: body(): lax.dot_general(dy_rows, hidden, row_dims, preferred_element_type=jnp.flo...]
  transfers between devices with their start and end apart: 5 -> 0, of which waited for: 2 -> 0; matrix products, arithmetic and copies ran while one was open for 1% -> 0% of each run, Pallas kernels for 0% -> 0%
where the time goes in v3:
time: 108 us
  Pallas kernels  102 us (94%)
  local copies, waits for them, and re-layouts  5.19 us (5%)
    pallas_call x1, Pallas kernels, body(): pl.pallas_call(functools.partial(kernel, (Y, Z, D, CA, RA)), out_shape=(j...  102 us
    unnamed x10, local copies, waits for them, and re-layouts  5.19 us

profile of v3, /device:TPU:1, one launch (start us, length us, event | category | flops | bytes accessed | tf_op | source)
XLA Modules:
  0.0 107.7 jit_solution(17622074984434970874)
XLA Ops:
  0.6 101.8 %shard_map.93 = (bf16[128,2048]{1,0:T(8,128)(2,1)}, bf16[2048,128]{1,0:T(8,128)(2,1)}, bf16[2048,128]{1,0:T(8,128)(2,1)}, bf16[2048,128]{1,0:T(8,128)(2,1)}) custom-call(s32[1,128]{1,0:T(1,128)} %ids_ref.1, bf16[128,2048]{1,0:T(8,128)(2,1)} %bitcast.13, bf16[128,2048]{1,0:T(8,128)(2,1)} %bitcast.14, bf16[2048,128]{1,0:T(8,128)(2,1)} %bitcast.15, ...), custom_call_target="tpu_custom_call" | custom-call | tf_op jit(solution)/shard_map/pallas_call | solution.py:451
  102.5 0.0 copy-start.2
  102.5 1.9 %copy.14 = bf16[1,128,2048]{2,1,0:T(8,128)(2,1)} copy(bf16[1,128,2048]{2,1,0:T(8,128)(2,1)} %bitcast.12) | data formatting | bytes 1048576
  104.4 0.0 copy-done.2
  104.4 0.0 copy-start.1
  104.4 0.8 copy.15
  105.2 0.4 copy-done.1
  105.6 0.0 copy-start
  105.6 0.8 copy.16
  106.4 0.4 copy-done
  106.9 0.8 copy.17
Async XLA Ops:
  102.5 2.0 %copy-start.2 = (bf16[2048,128]{1,0:T(8,128)(2,1)S(1)}, bf16[2048,128]{1,0:T(8,128)(2,1)}, u32[]{:S(2)}) copy-start(bf16[2048,128]{1,0:T(8,128)(2,1)} %get-tuple-element.9) | copy-start | bytes 1572868
  104.4 1.2 %copy-start.1 = (bf16[2048,128]{1,0:T(8,128)(2,1)S(1)}, bf16[2048,128]{1,0:T(8,128)(2,1)}, u32[]{:S(2)}) copy-start(bf16[2048,128]{1,0:T(8,128)(2,1)} %get-tuple-element.10) | copy-start | bytes 1572868
  105.6 1.2 %copy-start = (bf16[2048,128]{1,0:T(8,128)(2,1)S(1)}, bf16[2048,128]{1,0:T(8,128)(2,1)}, u32[]{:S(2)}) copy-start(bf16[2048,128]{1,0:T(8,128)(2,1)} %get-tuple-element.11) | copy-start | bytes 1572868

commit v4 on v3

v4 whole, which is shorter than its diff:
```python
import functools

import jax
import jax.numpy as jnp
from jax import lax
from jax.experimental import pallas as pl
from jax.experimental.pallas import tpu as pltpu
from jax.sharding import PartitionSpec as P

SLOT = 8
CUTS = 4
Z_HI = 2
F32 = jnp.float32
BF16 = jnp.bfloat16
ROWS_DIM = (((0,), (0,)), ((), ()))
BACK_DIM = (((1,), (1,)), ((), ()))


def slot_match(ids):
    tokens = ids.shape[1]
    chosen = jnp.broadcast_to((ids == 0).astype(F32), (SLOT, tokens))
    before = lax.broadcasted_iota(jnp.int32, (tokens, tokens), 0)
    after = lax.broadcasted_iota(jnp.int32, (tokens, tokens), 1)
    order = (before < after).astype(F32).astype(BF16)
    within = jnp.dot(chosen.astype(BF16), order, preferred_element_type=F32)
    place = lax.broadcasted_iota(jnp.int32, (SLOT, tokens), 0).astype(F32)
    return jnp.where(within == place, chosen, 0.0).astype(BF16)


def kernel(cfg, ids_ref, x_ref, dy_ref, wg_ref, wu_ref, wd_ref, og_ref, gg_ref, gu_ref, gd_ref,
           x_v, dy_v, w_gu, w_dn, shift_dy, shift_ids, g_a, g_b, x_all, dy_all, d_gu, hid, part,
           s_r, r_r, s_l, r_l, s_y, r_y, og_v, gg_v, gu_v, gd_v,
           loc, sh_s, sh_r, a1_s, a1_r, ar_s, ar_r, al_s, al_r, br_s, br_r, bl_s, bl_r, by_s, by_r,
           rr_s, rr_r, rl_s, rl_r, ry_s, ry_r):
    Y, Z, D, CA = cfg
    CW = D // CUTS
    K = Z // 2
    n_sec, n_exp = lax.axis_size("section"), lax.axis_size("expert")
    sec, ex, dp = lax.axis_index("section"), lax.axis_index("expert"), lax.axis_index("dp")
    y, z = dp // Z_HI, lax.rem(dp, Z_HI) * n_exp + ex

    def wrap(v, n):
        return lax.rem(v + n, n)

    def at(yy, zz):
        return {"expert": lax.rem(zz, n_exp), "dp": yy * Z_HI + zz // n_exp}

    z_right, z_left = at(y, wrap(z + 1, Z)), at(y, wrap(z - 1, Z))
    y_right, y_left = at(wrap(y + 1, Y), z), at(wrap(y - 1, Y), z)
    y_far = at(wrap(y + 2, Y), z)
    s_prev, s_next = wrap(sec - 1, n_sec), wrap(sec + 1, n_sec)
    turn = (0, 1, -1, 2)
    owners = [{"section": s_prev, **at(wrap(y + t, Y), z)} for t in turn]
    givers = [{"section": s_next, **at(wrap(y - t, Y), z)} for t in turn]

    def remote(src, dst, s_sem, r_sem, to):
        return pltpu.make_async_remote_copy(
            src_ref=src, dst_ref=dst, send_sem=s_sem, recv_sem=r_sem, device_id=to, device_id_type=pl.DeviceIdType.MESH)

    barrier = pltpu.get_barrier_semaphore()
    partners = [z_right, z_left, y_right, y_left, y_far] + givers
    for to in partners:
        pl.semaphore_signal(barrier, inc=1, device_id=to, device_id_type=pl.DeviceIdType.MESH)

    half = w_gu.shape[1] // 2
    loads = [
        pltpu.make_async_copy(x_ref, x_v, loc.at[0]),
        pltpu.make_async_copy(dy_ref, dy_v, loc.at[1]),
        pltpu.make_async_copy(wg_ref, w_gu.at[:, pl.ds(0, half)], loc.at[2]),
        pltpu.make_async_copy(wu_ref, w_gu.at[:, pl.ds(half, half)], loc.at[3]),
        pltpu.make_async_copy(wd_ref, w_dn, loc.at[4]),
    ]
    for copy in loads:
        copy.start()
    match = slot_match(ids_ref[...])
    loads[0].wait()
    loads[1].wait()
    own = jnp.concatenate([
        jnp.dot(match, x_v[...], preferred_element_type=F32),
        jnp.dot(match, dy_v[...], preferred_element_type=F32)], axis=0).astype(BF16)
    g_a[z, y] = own[:, :CA]
    g_b[z, y] = own[:, CA:]
    pl.semaphore_wait(barrier, len(partners))

    def a1(j, to):
        return remote(g_a.at[z, y], g_a.at[z, y], a1_s.at[j], a1_r.at[j], to)

    def a1_in(j, yy):
        return remote(g_a.at[z, yy], g_a.at[z, yy], a1_s.at[j], a1_r.at[j], y_right)

    def a_right(k, block, j):
        ref = g_a.at[block, wrap(y + turn[j], Y)]
        return remote(ref, ref, ar_s.at[k, j], ar_r.at[k, j], z_right)

    def a_left(k, block, j):
        ref = g_a.at[block, wrap(y + turn[j], Y)]
        return remote(ref, ref, al_s.at[k, j], al_r.at[k, j], z_left)

    def b_right(k, block):
        return remote(g_b.at[block, y], g_b.at[block, y], br_s.at[k], br_r.at[k], z_right)

    def b_left(k, block):
        return remote(g_b.at[block, y], g_b.at[block, y], bl_s.at[k], bl_r.at[k], z_left)

    def b_y(kind, o, yy, to):
        block = wrap(z - o, Z)
        return remote(g_b.at[block, yy], g_b.at[block, yy], by_s.at[kind, o], by_r.at[kind, o], to)

    def spread(o):
        b_y(0, o, y, y_right).start()
        b_y(1, o, y, y_left).start()

    for j, to in enumerate((y_right, y_left, y_far)):
        a1(j, to).start()
    b_right(0, z).start()
    b_left(0, z).start()
    spread(0)
    shift = [remote(ids_ref, shift_ids, sh_s.at[0], sh_r.at[0], owners[0]), remote(dy_ref, shift_dy, sh_s.at[1], sh_r.at[1], owners[0])]
    for copy in shift:
        copy.start()
    a_right(0, z, 0).start()
    a_left(0, z, 0).start()
    for j, came in ((1, 1), (2, 0), (3, 2)):
        a1_in(came, wrap(y + turn[j], Y)).wait_recv()
        a_right(0, z, j).start()
        a_left(0, z, j).start()

    def pass_right(o):
        b_y(0, o, wrap(y - 1, Y), y_right).wait_recv()
        b_y(2, o, wrap(y - 1, Y), y_right).start()

    def pass_left(o):
        b_y(1, o, wrap(y + 1, Y), y_left).wait_recv()
        b_y(2, o, wrap(y + 1, Y), y_left).start()

    def gather_step(k, _):
        zr, zl = wrap(z - k, Z), wrap(z + k, Z)

        @pl.when(k < K)
        def _():
            b_right(k - 1, zr).wait_recv()

            @pl.when(k < K - 1)
            def _():
                b_right(k, zr).start()

            spread(k)

        b_left(k - 1, zl).wait_recv()

        @pl.when(k < K)
        def _():
            b_left(k, zl).start()

        spread(Z - k)
        for j in range(Y):
            def right(j=j):
                a_right(k - 1, zr, j).wait_recv()

                @pl.when(k < (K if j < Y // 2 else K - 1))
                def _():
                    a_right(k, zr, j).start()

            def left(j=j):
                a_left(k - 1, zl, j).wait_recv()

                @pl.when(k < (K - 1 if j < Y // 2 else K))
                def _():
                    a_left(k, zl, j).start()

            if j < Y // 2:
                right()
                pl.when(k < K)(left)
            else:
                pl.when(k < K)(right)
                left()

        pass_right(k - 1)

        @pl.when(k > 1)
        def _():
            pass_left(Z - k + 1)

        return 0

    lax.fori_loop(1, K + 1, gather_step, 0)
    pass_left(K)

    def gather_end(o, _):
        @pl.when(o < K)
        def _():
            b_y(1, o, wrap(y + 1, Y), y_left).wait_recv()

        @pl.when(o >= K)
        def _():
            b_y(0, o, wrap(y - 1, Y), y_right).wait_recv()

        b_y(2, o, wrap(y + 2, Y), y_right).wait_recv()
        return 0

    lax.fori_loop(0, Z, gather_end, 0)
    for copy in loads[2:]:
        copy.wait()

    CZ = 128 // (Y * SLOT)

    def unpack(c, _):
        rows = pl.ds(pl.multiple_of(c * (Y * SLOT), Y * SLOT), Y * SLOT)
        for ref, lo, hi in ((g_a, 0, CA), (g_b, CA, D)):
            both = ref[c].astype(F32)
            x_all[rows, lo:hi] = both[:, :SLOT].reshape(Y * SLOT, hi - lo).astype(BF16)
            dy_all[rows, lo:hi] = both[:, SLOT:].reshape(Y * SLOT, hi - lo).astype(BF16)
        return 0

    lax.fori_loop(0, Z, unpack, 0)

    def forward(c, _):
        rows = pl.ds(pl.multiple_of(c * 128, 128), 128)
        both = jnp.dot(x_all[rows, :], w_gu[...], preferred_element_type=F32)
        d_hidden = jnp.dot(dy_all[rows, :], w_dn[...], preferred_element_type=F32)
        gate, upper = both[:, :half], both[:, half:]
        sigma = jax.nn.sigmoid(gate)
        active = gate * sigma
        hid[rows, :] = (active * upper).astype(BF16)
        d_gu[rows, :half] = (d_hidden * upper * sigma * (1.0 + gate * (1.0 - sigma))).astype(BF16)
        d_gu[rows, half:] = (d_hidden * active).astype(BF16)
        for cut in range(CUTS):
            piece = lax.dot_general(
                d_gu[rows, :], w_gu[cut * CW:(cut + 1) * CW, :], BACK_DIM, preferred_element_type=F32)
            part[pl.ds(c * CZ, CZ), cut] = piece.reshape(CZ, Y * SLOT, CW)
        return 0

    lax.fori_loop(0, Z // CZ, forward, 0)

    def to_right(k, cut):
        return remote(s_r.at[k, cut], r_r.at[k, cut], rr_s.at[k, cut], rr_r.at[k, cut], z_right)

    def to_left(k, cut):
        return remote(s_l.at[k, cut], r_l.at[k, cut], rl_s.at[k, cut], rl_r.at[k, cut], z_left)

    def add_right(k, cut, got):
        value = part[wrap(z + K - k, Z), cut]
        if got:
            to_right(k - 1, cut).wait_recv()
            value = value + r_r[k - 1, cut].astype(F32)
        s_r[k, cut] = value.astype(BF16)
        to_right(k, cut).start()

    def add_left(k, cut, got):
        value = part[wrap(z - K + k, Z), cut]
        if got:
            to_left(k - 1, cut).wait_recv()
            value = value + r_l[k - 1, cut].astype(F32)
        s_l[k, cut] = value.astype(BF16)
        to_left(k, cut).start()

    WD = D // K

    def weights(j):
        cols = pl.ds(pl.multiple_of(j * WD, WD), WD)
        both = lax.dot_general(x_all[:, cols], d_gu[...], ROWS_DIM, preferred_element_type=F32).astype(BF16)
        gg_v[cols, :] = both[:, :half]
        gu_v[cols, :] = both[:, half:]
        gd_v[cols, :] = lax.dot_general(dy_all[:, cols], hid[...], ROWS_DIM, preferred_element_type=F32).astype(BF16)

    first, second = range(CUTS // 2), range(CUTS // 2, CUTS)
    for cut in first:
        add_right(0, cut, False)
    for cut in second:
        add_left(0, cut, False)
    for cut in second:
        add_right(1, cut, False)
    for cut in first:
        add_left(1, cut, False)
    weights(0)
    for a, b in zip(first, second):
        add_right(1, a, True)
        add_left(1, b, True)
    weights(1)

    def reduce_step(k, _):
        for a, b in zip(list(second) + list(first), list(first) + list(second)):
            add_right(k, a, True)
            add_left(k, b, True)
        weights(k)
        return 0

    lax.fori_loop(2, K, reduce_step, 0)
    outs = [
        pltpu.make_async_copy(gg_v, gg_ref, loc.at[0]),
        pltpu.make_async_copy(gu_v, gu_ref, loc.at[1]),
        pltpu.make_async_copy(gd_v, gd_ref, loc.at[2]),
    ]
    for copy in outs:
        copy.start()

    def to_owner(j):
        yy = wrap(y + turn[j], Y)
        return remote(s_y.at[yy], r_y.at[j], ry_s.at[j], ry_r.at[j], owners[j])

    for a, b in zip(list(second) + list(first), list(first) + list(second)):
        to_right(K - 1, a).wait_recv()
        to_left(K - 1, b).wait_recv()
    for cut in range(CUTS):
        total = part[z, cut] + r_r[K - 1, cut].astype(F32) + r_l[K - 1, cut].astype(F32)
        total = total.reshape(Y, SLOT, CW)
        total = jnp.concatenate([total[:, :, :CW // 2], total[:, :, CW // 2:]], axis=1).astype(BF16)
        s_y[:, cut] = total
    for j in (3, 1, 2, 0):
        to_owner(j).start()
    for copy in shift:
        copy.wait_recv()
    match = slot_match(shift_ids[...])
    for j in range(Y):
        to_owner(j).wait_recv()
    for cut in range(CUTS):
        rows = r_y[0, cut].astype(F32)
        for j in range(1, Y):
            rows = rows + r_y[j, cut].astype(F32)
        rows = jnp.concatenate([rows[:SLOT], rows[SLOT:]], axis=1).astype(BF16)
        term = lax.dot_general(match, rows, ROWS_DIM, preferred_element_type=F32)
        cols = slice(cut * CW, (cut + 1) * CW)
        og_v[:, cols] = (shift_dy[:, cols].astype(F32) + term).astype(BF16)
    last = pltpu.make_async_copy(og_v, og_ref, loc.at[3])
    last.start()

    for copy in shift:
        copy.wait_send()
    for j, to in enumerate((y_right, y_left, y_far)):
        a1(j, to).wait_send()
    for j in range(Y):
        to_owner(j).wait_send()

    def sent(k, _):
        for j in range(Y):
            pl.when(k < (K if j < Y // 2 else K - 1))(lambda j=j: a_right(k, z, j).wait_send())
            pl.when(k < (K - 1 if j < Y // 2 else K))(lambda j=j: a_left(k, z, j).wait_send())
        b_left(k, z).wait_send()
        pl.when(k < K - 1)(lambda: b_right(k, z).wait_send())
        for cut in range(CUTS):
            if cut in first:
                to_right(k, cut).wait_send()
                pl.when(k > 0)(lambda cut=cut: to_left(k, cut).wait_send())
            else:
                to_left(k, cut).wait_send()
                pl.when(k > 0)(lambda cut=cut: to_right(k, cut).wait_send())
        for kind in range(3):
            b_y(kind, k, y, y_right).wait_send()
            b_y(kind, K + k, y, y_right).wait_send()
        return 0

    lax.fori_loop(0, K, sent, 0)
    for copy in outs + [last]:
        copy.wait()


def handout(*refs):
    for source, target in zip(refs[:4], refs[4:]):
        target[...] = source[...]


def split(width):
    unit = 256
    return max(unit, (width * 3 // 8) // unit * unit)


def body(Z_AXIS, layer_input, output_grad, expert_ids, w_gate, w_up, w_down):
    Y, Z = Z_AXIS
    _, tokens, D = layer_input.shape
    hidden = w_gate.shape[2]
    CA = split(D)
    K = Z // 2
    rows = Y * Z * SLOT
    CB, CW = D - CA, D // CUTS
    V, DMA = pltpu.VMEM, pltpu.SemaphoreType.DMA
    scratch = [
        V((tokens, D), BF16), V((tokens, D), BF16), V((D, 2 * hidden), BF16), V((D, hidden), BF16),
        V((tokens, D), BF16), V((1, tokens), jnp.int32),
        V((Z, Y, 2 * SLOT, CA), BF16), V((Z, Y, 2 * SLOT, CB), BF16),
        V((rows, D), BF16), V((rows, D), BF16), V((rows, 2 * hidden), BF16), V((rows, hidden), BF16),
        V((Z, CUTS, Y * SLOT, CW), F32),
        *[V((K, CUTS, Y * SLOT, CW), BF16)] * 4,
        *[V((Y, CUTS, 2 * SLOT, CW // 2), BF16)] * 2,
        V((tokens, D), BF16), V((D, hidden), BF16), V((D, hidden), BF16), V((D, hidden), BF16),
        DMA((5,)), DMA((2,)), DMA((2,)), DMA((3,)), DMA((3,)),
        *[DMA((K, Y))] * 4, *[DMA((K,))] * 4, DMA((3, Z)), DMA((3, Z)),
        *[DMA((K, CUTS))] * 4, DMA((Y,)), DMA((Y,)),
    ]
    anywhere = pl.BlockSpec(memory_space=pl.ANY)
    weight = jax.ShapeDtypeStruct((D, hidden), BF16)
    token_grad, grad_gate, grad_up, grad_down = pl.pallas_call(
        functools.partial(kernel, (Y, Z, D, CA)),
        out_shape=(jax.ShapeDtypeStruct((tokens, D), BF16), weight, weight, weight),
        in_specs=[pl.BlockSpec(memory_space=pltpu.VMEM)] + [anywhere] * 5,
        out_specs=(anywhere,) * 4,
        scratch_shapes=scratch,
        compiler_params=pltpu.CompilerParams(collective_id=0, has_side_effects=True, vmem_limit_bytes=56 << 20),
    )(expert_ids, layer_input[0], output_grad[0], w_gate[0], w_up[0], w_down[0])
    steps = 4
    blocks = [pl.BlockSpec((n // steps, m), lambda i: (i, 0)) for n, m in ((tokens, D),) + ((D, hidden),) * 3]
    token_grad, grad_gate, grad_up, grad_down = pl.pallas_call(
        handout,
        grid=(steps,),
        out_shape=(jax.ShapeDtypeStruct((tokens, D), BF16), weight, weight, weight),
        in_specs=blocks,
        out_specs=blocks,
    )(token_grad, grad_gate, grad_up, grad_down)
    return token_grad[None], grad_gate[None], grad_up[None], grad_down[None]


def solution(mesh):
    rows = P("section", ("expert", "dp"), None)
    weights = P("section", None, ("expert", "dp"))
    in_specs = (rows, rows, P("section", ("expert", "dp")), weights, weights, weights)
    out_specs = (rows, weights, weights, weights)
    size = (mesh.shape["dp"] // Z_HI, mesh.shape["expert"] * Z_HI)
    return jax.shard_map(functools.partial(body, size), mesh=mesh, in_specs=in_specs, out_specs=out_specs, check_vma=False)
```

time: 108 us -> 94.5 us (0.88)
  Pallas kernels: 102 us -> 93.6 us
  local copies, waits for them, and re-layouts: 5.19 us -> 0 us
    pallas_call x1 -> x2, Pallas kernels: 102 us -> 93.6 us  [the longest x1 89.8 us: body(): pl.pallas_call(functools.partial(kernel, (Y, Z, D, CA)), out_shape=(jax.S...]
    unnamed x10 -> x0, local copies, waits for them, and re-layouts: 5.19 us -> none
where the time goes in v4:
time: 94.5 us; the launch traced here: 94.3 us
  Pallas kernels  93.6 us (99%)
    pallas_call x1, Pallas kernels, body(): pl.pallas_call(functools.partial(kernel, (Y, Z, D, CA)), out_shape=(jax.S...  89.8 us
    pallas_call x1, Pallas kernels, body(): pl.pallas_call(handout, grid=(steps,), out_shape=(jax.ShapeDtypeStruct((t...  3.81 us

profile of v4, /device:TPU:1, one launch (start us, length us, event | category | flops | bytes accessed | tf_op | source)
XLA Modules:
  0.0 94.3 jit_solution(1006864916035713666)
XLA Ops:
  0.6 89.8 %shard_map.93 = (bf16[128,2048]{1,0:T(8,128)(2,1)}, bf16[2048,128]{1,0:T(8,128)(2,1)}, bf16[2048,128]{1,0:T(8,128)(2,1)}, bf16[2048,128]{1,0:T(8,128)(2,1)}) custom-call(s32[1,128]{1,0:T(1,128)} %ids_ref.1, bf16[128,2048]{1,0:T(8,128)(2,1)} %bitcast.9, bf16[128,2048]{1,0:T(8,128)(2,1)} %bitcast.10, bf16[2048,128]{1,0:T(8,128)(2,1)} %bitcast.11, ...), custom_call_target="tpu_custom_call" | custom-call | tf_op jit(solution)/shard_map/pallas_call | solution.py:391
  90.5 3.8 %shard_map.94 = (bf16[128,2048]{1,0:T(8,128)(2,1)}, bf16[2048,128]{1,0:T(8,128)(2,1)}, bf16[2048,128]{1,0:T(8,128)(2,1)}, bf16[2048,128]{1,0:T(8,128)(2,1)}) custom-call(bf16[128,2048]{1,0:T(8,128)(2,1)} %get-tuple-element.12.refs_0_, bf16[2048,128]{1,0:T(8,128)(2,1)} %get-tuple-element.13.refs_1_, bf16[2048,128]{1,0:T(8,128)(2,1)} %get-tuple-element.14.refs_2_, ...), custom_call_target="tpu_custom_call" | custom-call | tf_op jit(solution)/shard_map/pallas_call | solution.py:401

commit v5 on v4

--- a/solution.py
+++ b/solution.py
@@ -9,6 +9,7 @@
 
 SLOT = 8
 CUTS = 4
+QUARTERS = 4
 Z_HI = 2
 F32 = jnp.float32
 BF16 = jnp.bfloat16
@@ -133,89 +134,35 @@
         b_y(1, o, wrap(y + 1, Y), y_left).wait_recv()
         b_y(2, o, wrap(y + 1, Y), y_left).start()
 
-    def gather_step(k, _):
-        zr, zl = wrap(z - k, Z), wrap(z + k, Z)
-
-        @pl.when(k < K)
-        def _():
-            b_right(k - 1, zr).wait_recv()
-
-            @pl.when(k < K - 1)
+    CZ = Z // QUARTERS
+    QR = CZ * Y * SLOT
+
+    def quarter(i):
+        rows = pl.ds(pl.multiple_of(i * QR, QR), QR)
+
+        def unpack(n, _):
+            place = i * CZ + n
+            away = lax.rem(place, 2) * (place + 1) // 2 - (1 - lax.rem(place, 2)) * (place // 2)
+            block = wrap(z + away, Z)
+            o = wrap(-away, Z)
+
+            @pl.when(o < K)
             def _():
-                b_right(k, zr).start()
-
-            spread(k)
-
-        b_left(k - 1, zl).wait_recv()
-
-        @pl.when(k < K)
-        def _():
-            b_left(k, zl).start()
-
-        spread(Z - k)
-        for j in range(Y):
-            def right(j=j):
-                a_right(k - 1, zr, j).wait_recv()
-
-                @pl.when(k < (K if j < Y // 2 else K - 1))
-                def _():
-                    a_right(k, zr, j).start()
-
-            def left(j=j):
-                a_left(k - 1, zl, j).wait_recv()
-
-                @pl.when(k < (K - 1 if j < Y // 2 else K))
-                def _():
-                    a_left(k, zl, j).start()
-
-            if j < Y // 2:
-                right()
-                pl.when(k < K)(left)
-            else:
-                pl.when(k < K)(right)
-                left()
-
-        pass_right(k - 1)
-
-        @pl.when(k > 1)
-        def _():
-            pass_left(Z - k + 1)
-
-        return 0
-
-    lax.fori_loop(1, K + 1, gather_step, 0)
-    pass_left(K)
-
-    def gather_end(o, _):
-        @pl.when(o < K)
-        def _():
-            b_y(1, o, wrap(y + 1, Y), y_left).wait_recv()
-
-        @pl.when(o >= K)
-        def _():
-            b_y(0, o, wrap(y - 1, Y), y_right).wait_recv()
-
-        b_y(2, o, wrap(y + 2, Y), y_right).wait_recv()
-        return 0
-
-    lax.fori_loop(0, Z, gather_end, 0)
-    for copy in loads[2:]:
-        copy.wait()
-
-    CZ = 128 // (Y * SLOT)
-
-    def unpack(c, _):
-        rows = pl.ds(pl.multiple_of(c * (Y * SLOT), Y * SLOT), Y * SLOT)
-        for ref, lo, hi in ((g_a, 0, CA), (g_b, CA, D)):
-            both = ref[c].astype(F32)
-            x_all[rows, lo:hi] = both[:, :SLOT].reshape(Y * SLOT, hi - lo).astype(BF16)
-            dy_all[rows, lo:hi] = both[:, SLOT:].reshape(Y * SLOT, hi - lo).astype(BF16)
-        return 0
-
-    lax.fori_loop(0, Z, unpack, 0)
-
-    def forward(c, _):
-        rows = pl.ds(pl.multiple_of(c * 128, 128), 128)
+                b_y(1, o, wrap(y + 1, Y), y_left).wait_recv()
+
+            @pl.when(o >= K)
+            def _():
+                b_y(0, o, wrap(y - 1, Y), y_right).wait_recv()
+
+            b_y(2, o, wrap(y + 2, Y), y_right).wait_recv()
+            here = pl.ds(pl.multiple_of(place * (Y * SLOT), Y * SLOT), Y * SLOT)
+            for ref, lo, hi in ((g_a, 0, CA), (g_b, CA, D)):
+                both = ref[block].astype(F32)
+                x_all[here, lo:hi] = both[:, :SLOT].reshape(Y * SLOT, hi - lo).astype(BF16)
+                dy_all[here, lo:hi] = both[:, SLOT:].reshape(Y * SLOT, hi - lo).astype(BF16)
+            return 0
+
+        lax.fori_loop(0, CZ, unpack, 0)
         both = jnp.dot(x_all[rows, :], w_gu[...], preferred_element_type=F32)
         d_hidden = jnp.dot(dy_all[rows, :], w_dn[...], preferred_element_type=F32)
         gate, upper = both[:, :half], both[:, half:]
@@ -227,10 +174,74 @@
         for cut in range(CUTS):
             piece = lax.dot_general(
                 d_gu[rows, :], w_gu[cut * CW:(cut + 1) * CW, :], BACK_DIM, preferred_element_type=F32)
-            part[pl.ds(c * CZ, CZ), cut] = piece.reshape(CZ, Y * SLOT, CW)
+            part[pl.ds(i * CZ, CZ), cut] = piece.reshape(CZ, Y * SLOT, CW)
+
+    def gather_step(k, _):
+        zr, zl = wrap(z - k, Z), wrap(z + k, Z)
+
+        @pl.when(k < K)
+        def _():
+            b_right(k - 1, zr).wait_recv()
+
+            @pl.when(k < K - 1)
+            def _():
+                b_right(k, zr).start()
+
+            spread(k)
+
+        b_left(k - 1, zl).wait_recv()
+
+        @pl.when(k < K)
+        def _():
+            b_left(k, zl).start()
+
+        spread(Z - k)
+        for j in range(Y):
+            def right(j=j):
+                a_right(k - 1, zr, j).wait_recv()
+
+                @pl.when(k < (K if j < Y // 2 else K - 1))
+                def _():
+                    a_right(k, zr, j).start()
+
+            def left(j=j):
+                a_left(k - 1, zl, j).wait_recv()
+
+                @pl.when(k < (K - 1 if j < Y // 2 else K))
+                def _():
+                    a_left(k, zl, j).start()
+
+            if j < Y // 2:
+                right()
+                pl.when(k < K)(left)
+            else:
+                pl.when(k < K)(right)
+                left()
+
+        pass_right(k - 1)
+
+        @pl.when(k > 1)
+        def _():
+            pass_left(Z - k + 1)
+
+        early = K // 2 + 1
+
+        if K == 2 * QUARTERS:
+            @pl.when((k >= early) & (lax.rem(k - early, 2) == 0) & (k < K))
+            def _():
+                quarter((k - early) // 2)
+
         return 0
 
-    lax.fori_loop(0, Z // CZ, forward, 0)
+    for copy in loads[2:]:
+        copy.wait()
+    lax.fori_loop(1, K + 1, gather_step, 0)
+    pass_left(K)
+    if K != 2 * QUARTERS:
+        for i in range(QUARTERS - 1):
+            quarter(i)
+
+    quarter(QUARTERS - 1)
 
     def to_right(k, cut):
         return remote(s_r.at[k, cut], r_r.at[k, cut], rr_s.at[k, cut], rr_r.at[k, cut], z_right)
@@ -239,7 +250,7 @@
         return remote(s_l.at[k, cut], r_l.at[k, cut], rl_s.at[k, cut], rl_r.at[k, cut], z_left)
 
     def add_right(k, cut, got):
-        value = part[wrap(z + K - k, Z), cut]
+        value = part[2 * (K - k) - 1, cut]
         if got:
             to_right(k - 1, cut).wait_recv()
             value = value + r_r[k - 1, cut].astype(F32)
@@ -247,7 +258,7 @@
         to_right(k, cut).start()
 
     def add_left(k, cut, got):
-        value = part[wrap(z - K + k, Z), cut]
+        value = part[2 * (K - k) - (1 if isinstance(k, int) and k == 0 else 0), cut]
         if got:
             to_left(k - 1, cut).wait_recv()
             value = value + r_l[k - 1, cut].astype(F32)
@@ -272,10 +283,12 @@
         add_right(1, cut, False)
     for cut in first:
         add_left(1, cut, False)
-    weights(0)
+    if K == 2 * QUARTERS:
+        quarter(QUARTERS - 2)
     for a, b in zip(first, second):
         add_right(1, a, True)
         add_left(1, b, True)
+    weights(0)
     weights(1)
 
     def reduce_step(k, _):
@@ -302,7 +315,7 @@
         to_right(K - 1, a).wait_recv()
         to_left(K - 1, b).wait_recv()
     for cut in range(CUTS):
-        total = part[z, cut] + r_r[K - 1, cut].astype(F32) + r_l[K - 1, cut].astype(F32)
+        total = part[0, cut] + r_r[K - 1, cut].astype(F32) + r_l[K - 1, cut].astype(F32)
         total = total.reshape(Y, SLOT, CW)
         total = jnp.concatenate([total[:, :, :CW // 2], total[:, :, CW // 2:]], axis=1).astype(BF16)
         s_y[:, cut] = total

time: 94.5 us -> 91.8 us (0.971)
  Pallas kernels: 93.6 us -> 91 us
    pallas_call x1, Pallas kernels: 89.8 us -> 87.2 us  [body(): pl.pallas_call(functools.partial(kernel, (Y, Z, D, CA)), out_shape=(jax.S...]
where the time goes in v5:
time: 91.8 us; the launch traced here: 91.6 us
  Pallas kernels  91 us (99%)
    pallas_call x1, Pallas kernels, body(): pl.pallas_call(functools.partial(kernel, (Y, Z, D, CA)), out_shape=(jax.S...  87.2 us
    pallas_call x1, Pallas kernels, body(): pl.pallas_call(handout, grid=(steps,), out_shape=(jax.ShapeDtypeStruct((t...  3.81 us

profile of v5, /device:TPU:1, one launch (start us, length us, event | category | flops | bytes accessed | tf_op | source)
XLA Modules:
  0.0 91.6 jit_solution(2477040202140717371)
XLA Ops:
  0.6 87.2 %shard_map.93 = (bf16[128,2048]{1,0:T(8,128)(2,1)}, bf16[2048,128]{1,0:T(8,128)(2,1)}, bf16[2048,128]{1,0:T(8,128)(2,1)}, bf16[2048,128]{1,0:T(8,128)(2,1)}) custom-call(s32[1,128]{1,0:T(1,128)} %ids_ref.1, bf16[128,2048]{1,0:T(8,128)(2,1)} %bitcast.9, bf16[128,2048]{1,0:T(8,128)(2,1)} %bitcast.10, bf16[2048,128]{1,0:T(8,128)(2,1)} %bitcast.11, ...), custom_call_target="tpu_custom_call" | custom-call | tf_op jit(solution)/shard_map/pallas_call | solution.py:404
  87.8 3.8 %shard_map.94 = (bf16[128,2048]{1,0:T(8,128)(2,1)}, bf16[2048,128]{1,0:T(8,128)(2,1)}, bf16[2048,128]{1,0:T(8,128)(2,1)}, bf16[2048,128]{1,0:T(8,128)(2,1)}) custom-call(bf16[128,2048]{1,0:T(8,128)(2,1)} %get-tuple-element.12.refs_0_, bf16[2048,128]{1,0:T(8,128)(2,1)} %get-tuple-element.13.refs_1_, bf16[2048,128]{1,0:T(8,128)(2,1)} %get-tuple-element.14.refs_2_, ...), custom_call_target="tpu_custom_call" | custom-call | tf_op jit(solution)/shard_map/pallas_call | solution.py:414

commit v6 on v5

--- a/solution.py
+++ b/solution.py
@@ -9,6 +9,7 @@
 
 SLOT = 8
 CUTS = 4
+RING = 3
 QUARTERS = 4
 Z_HI = 2
 F32 = jnp.float32
@@ -29,10 +30,10 @@
 
 
 def kernel(cfg, ids_ref, x_ref, dy_ref, wg_ref, wu_ref, wd_ref, og_ref, gg_ref, gu_ref, gd_ref,
-           x_v, dy_v, w_gu, w_dn, shift_dy, shift_ids, g_a, g_b, x_all, dy_all, d_gu, hid, part,
-           s_r, r_r, s_l, r_l, s_y, r_y, og_v, gg_v, gu_v, gd_v,
+           x_v, dy_v, w_gu, w_dn, shift_dy, shift_ids, g_a, g_b, x_all, dy_all, d_gu, hid, part, part_y,
+           s_r, r_r, s_l, r_l, s_y, r_y, s_q, r_q, s_br, r_br, s_bl, r_bl, s_f, r_f, og_v, gg_v, gu_v, gd_v,
            loc, sh_s, sh_r, a1_s, a1_r, ar_s, ar_r, al_s, al_r, br_s, br_r, bl_s, bl_r, by_s, by_r,
-           rr_s, rr_r, rl_s, rl_r, ry_s, ry_r):
+           rr_s, rr_r, rl_s, rl_r, ry_s, ry_r, q_s, q_r, tr_s, tr_r, tl_s, tl_r, f_s, f_r):
     Y, Z, D, CA = cfg
     CW = D // CUTS
     K = Z // 2
@@ -137,6 +138,13 @@
     CZ = Z // QUARTERS
     QR = CZ * Y * SLOT
 
+    def swap(i, j):
+        return remote(s_q.at[i, j], r_q.at[i, j], q_s.at[i, j], q_r.at[i, j], (y_right, y_left, y_far)[j])
+
+    def swapped(i):
+        for j in range(Y - 1):
+            swap(i, j).wait_recv()
+
     def quarter(i):
         rows = pl.ds(pl.multiple_of(i * QR, QR), QR)
 
@@ -171,10 +179,19 @@
         hid[rows, :] = (active * upper).astype(BF16)
         d_gu[rows, :half] = (d_hidden * upper * sigma * (1.0 + gate * (1.0 - sigma))).astype(BF16)
         d_gu[rows, half:] = (d_hidden * active).astype(BF16)
-        for cut in range(CUTS):
+        for cut in range(CUTS - 1, -1, -1):
             piece = lax.dot_general(
                 d_gu[rows, :], w_gu[cut * CW:(cut + 1) * CW, :], BACK_DIM, preferred_element_type=F32)
-            part[pl.ds(i * CZ, CZ), cut] = piece.reshape(CZ, Y * SLOT, CW)
+            if cut < RING:
+                part[pl.ds(i * CZ, CZ), cut] = piece.reshape(CZ, Y * SLOT, CW)
+            else:
+                piece = piece.reshape(CZ, Y, SLOT, CW)
+                part_y[pl.ds(i * CZ, CZ)] = jnp.concatenate([piece[..., :CW // 2], piece[..., CW // 2:]], axis=2)
+                for j in (2, 0, 1):
+                    yy = wrap(y + turn[j + 1], Y)
+                    for n in range(CZ):
+                        s_q[i, j, n] = part_y[i * CZ + n, yy].astype(BF16)
+                    swap(i, j).start()
 
     def gather_step(k, _):
         zr, zl = wrap(z - k, Z), wrap(z + k, Z)
@@ -274,7 +291,34 @@
         gu_v[cols, :] = both[:, half:]
         gd_v[cols, :] = lax.dot_general(dy_all[:, cols], hid[...], ROWS_DIM, preferred_element_type=F32).astype(BF16)
 
-    first, second = range(CUTS // 2), range(CUTS // 2, CUTS)
+    def tall_right(k):
+        return remote(s_br.at[k], r_br.at[k], tr_s.at[k], tr_r.at[k], z_right)
+
+    def tall_left(k):
+        return remote(s_bl.at[k], r_bl.at[k], tl_s.at[k], tl_r.at[k], z_left)
+
+    def over_y(place):
+        value = part_y[place, y]
+        for j in range(Y - 1):
+            value = value + r_q[place // CZ, j, lax.rem(place, CZ)].astype(F32)
+        return value
+
+    def add_tall(k, right, left):
+        if right is not None:
+            value = over_y(2 * (K - k) - 1)
+            if right:
+                tall_right(k - 1).wait_recv()
+                value = value + r_br[k - 1].astype(F32)
+            s_br[k] = value.astype(BF16)
+            tall_right(k).start()
+        value = over_y(2 * (K - k) - (1 if isinstance(k, int) and k == 0 else 0))
+        if left:
+            tall_left(k - 1).wait_recv()
+            value = value + r_bl[k - 1].astype(F32)
+        s_bl[k] = value.astype(BF16)
+        tall_left(k).start()
+
+    first, second = range((RING + 1) // 2), range((RING + 1) // 2, RING)
     for cut in first:
         add_right(0, cut, False)
     for cut in second:
@@ -283,18 +327,28 @@
         add_right(1, cut, False)
     for cut in first:
         add_left(1, cut, False)
+    swapped(QUARTERS - 1)
+    if K != 2 * QUARTERS:
+        for i in range(QUARTERS - 1):
+            swapped(i)
+    add_tall(0, None, False)
     if K == 2 * QUARTERS:
         quarter(QUARTERS - 2)
-    for a, b in zip(first, second):
-        add_right(1, a, True)
-        add_left(1, b, True)
+    for cut in first:
+        add_right(1, cut, True)
+    for cut in second:
+        add_left(1, cut, True)
+    add_tall(1, False, True)
     weights(0)
     weights(1)
 
     def reduce_step(k, _):
-        for a, b in zip(list(second) + list(first), list(first) + list(second)):
-            add_right(k, a, True)
-            add_left(k, b, True)
+        for cut in range(RING):
+            add_right(k, RING - 1 - cut, True)
+            add_left(k, cut, True)
+        if K == 2 * QUARTERS:
+            pl.when(lax.rem(k, 2) == 0)(lambda: swapped((K - k) // 2 - 1))
+        add_tall(k, True, True)
         weights(k)
         return 0
 
@@ -311,25 +365,34 @@
         yy = wrap(y + turn[j], Y)
         return remote(s_y.at[yy], r_y.at[j], ry_s.at[j], ry_r.at[j], owners[j])
 
-    for a, b in zip(list(second) + list(first), list(first) + list(second)):
-        to_right(K - 1, a).wait_recv()
-        to_left(K - 1, b).wait_recv()
-    for cut in range(CUTS):
+    for cut in range(RING):
+        to_right(K - 1, RING - 1 - cut).wait_recv()
+        to_left(K - 1, cut).wait_recv()
+    for cut in range(RING):
         total = part[0, cut] + r_r[K - 1, cut].astype(F32) + r_l[K - 1, cut].astype(F32)
         total = total.reshape(Y, SLOT, CW)
         total = jnp.concatenate([total[:, :, :CW // 2], total[:, :, CW // 2:]], axis=1).astype(BF16)
         s_y[:, cut] = total
     for j in (3, 1, 2, 0):
         to_owner(j).start()
+    tall_right(K - 1).wait_recv()
+    tall_left(K - 1).wait_recv()
+    s_f[...] = (over_y(0) + r_br[K - 1].astype(F32) + r_bl[K - 1].astype(F32)).astype(BF16)
+    whole = remote(s_f, r_f, f_s.at[0], f_r.at[0], owners[0])
+    whole.start()
     for copy in shift:
         copy.wait_recv()
     match = slot_match(shift_ids[...])
     for j in range(Y):
         to_owner(j).wait_recv()
     for cut in range(CUTS):
-        rows = r_y[0, cut].astype(F32)
-        for j in range(1, Y):
-            rows = rows + r_y[j, cut].astype(F32)
+        if cut < RING:
+            rows = r_y[0, cut].astype(F32)
+            for j in range(1, Y):
+                rows = rows + r_y[j, cut].astype(F32)
+        else:
+            whole.wait_recv()
+            rows = r_f[...].astype(F32)
         rows = jnp.concatenate([rows[:SLOT], rows[SLOT:]], axis=1).astype(BF16)
         term = lax.dot_general(match, rows, ROWS_DIM, preferred_element_type=F32)
         cols = slice(cut * CW, (cut + 1) * CW)
@@ -343,6 +406,10 @@
         a1(j, to).wait_send()
     for j in range(Y):
         to_owner(j).wait_send()
+    whole.wait_send()
+    for i in range(QUARTERS):
+        for j in range(Y - 1):
+            swap(i, j).wait_send()
 
     def sent(k, _):
         for j in range(Y):
@@ -350,7 +417,9 @@
             pl.when(k < (K - 1 if j < Y // 2 else K))(lambda j=j: a_left(k, z, j).wait_send())
         b_left(k, z).wait_send()
         pl.when(k < K - 1)(lambda: b_right(k, z).wait_send())
-        for cut in range(CUTS):
+        tall_left(k).wait_send()
+        pl.when(k > 0)(lambda: tall_right(k).wait_send())
+        for cut in range(RING):
             if cut in first:
                 to_right(k, cut).wait_send()
                 pl.when(k > 0)(lambda cut=cut: to_left(k, cut).wait_send())
@@ -391,13 +460,17 @@
         V((tokens, D), BF16), V((1, tokens), jnp.int32),
         V((Z, Y, 2 * SLOT, CA), BF16), V((Z, Y, 2 * SLOT, CB), BF16),
         V((rows, D), BF16), V((rows, D), BF16), V((rows, 2 * hidden), BF16), V((rows, hidden), BF16),
-        V((Z, CUTS, Y * SLOT, CW), F32),
-        *[V((K, CUTS, Y * SLOT, CW), BF16)] * 4,
-        *[V((Y, CUTS, 2 * SLOT, CW // 2), BF16)] * 2,
+        V((Z, RING, Y * SLOT, CW), F32), V((Z, Y, 2 * SLOT, CW // 2), F32),
+        *[V((K, RING, Y * SLOT, CW), BF16)] * 4,
+        *[V((Y, RING, 2 * SLOT, CW // 2), BF16)] * 2,
+        *[V((QUARTERS, Y - 1, Z // QUARTERS, 2 * SLOT, CW // 2), BF16)] * 2,
+        *[V((K, 2 * SLOT, CW // 2), BF16)] * 4,
+        *[V((2 * SLOT, CW // 2), BF16)] * 2,
         V((tokens, D), BF16), V((D, hidden), BF16), V((D, hidden), BF16), V((D, hidden), BF16),
         DMA((5,)), DMA((2,)), DMA((2,)), DMA((3,)), DMA((3,)),
         *[DMA((K, Y))] * 4, *[DMA((K,))] * 4, DMA((3, Z)), DMA((3, Z)),
-        *[DMA((K, CUTS))] * 4, DMA((Y,)), DMA((Y,)),
+        *[DMA((K, RING))] * 4, DMA((Y,)), DMA((Y,)),
+        *[DMA((QUARTERS, Y - 1))] * 2, *[DMA((K,))] * 4, DMA((1,)), DMA((1,)),
     ]
     anywhere = pl.BlockSpec(memory_space=pl.ANY)
     weight = jax.ShapeDtypeStruct((D, hidden), BF16)

time: 91.8 us -> 94.3 us (1.027)
  Pallas kernels: 91 us -> 93.4 us
    pallas_call x1, Pallas kernels: 87.2 us -> 89.6 us  [body(): pl.pallas_call(functools.partial(kernel, (Y, Z, D, CA)), out_shape=(jax.S...]
where the time goes in v6:
time: 94.3 us; the launch traced here: 94.1 us
  Pallas kernels  93.4 us (99%)
    pallas_call x1, Pallas kernels, body(): pl.pallas_call(functools.partial(kernel, (Y, Z, D, CA)), out_shape=(jax.S...  89.6 us
    pallas_call x1, Pallas kernels, body(): pl.pallas_call(handout, grid=(steps,), out_shape=(jax.ShapeDtypeStruct((t...  3.81 us

profile of v6, /device:TPU:1, one launch (start us, length us, event | category | flops | bytes accessed | tf_op | source)
XLA Modules:
  0.0 94.1 jit_solution(18225296559045334622)
XLA Ops:
  0.6 89.6 %shard_map.93 = (bf16[128,2048]{1,0:T(8,128)(2,1)}, bf16[2048,128]{1,0:T(8,128)(2,1)}, bf16[2048,128]{1,0:T(8,128)(2,1)}, bf16[2048,128]{1,0:T(8,128)(2,1)}) custom-call(s32[1,128]{1,0:T(1,128)} %ids_ref.1, bf16[128,2048]{1,0:T(8,128)(2,1)} %bitcast.9, bf16[128,2048]{1,0:T(8,128)(2,1)} %bitcast.10, bf16[2048,128]{1,0:T(8,128)(2,1)} %bitcast.11, ...), custom_call_target="tpu_custom_call" | custom-call | tf_op jit(solution)/shard_map/pallas_call | solution.py:477
  90.2 3.8 %shard_map.94 = (bf16[128,2048]{1,0:T(8,128)(2,1)}, bf16[2048,128]{1,0:T(8,128)(2,1)}, bf16[2048,128]{1,0:T(8,128)(2,1)}, bf16[2048,128]{1,0:T(8,128)(2,1)}) custom-call(bf16[128,2048]{1,0:T(8,128)(2,1)} %get-tuple-element.12.refs_0_, bf16[2048,128]{1,0:T(8,128)(2,1)} %get-tuple-element.13.refs_1_, bf16[2048,128]{1,0:T(8,128)(2,1)} %get-tuple-element.14.refs_2_, ...), custom_call_target="tpu_custom_call" | custom-call | tf_op jit(solution)/shard_map/pallas_call | solution.py:487

commit v7 on v5

--- a/solution.py
+++ b/solution.py
@@ -28,9 +28,9 @@
     return jnp.where(within == place, chosen, 0.0).astype(BF16)
 
 
-def kernel(cfg, ids_ref, x_ref, dy_ref, wg_ref, wu_ref, wd_ref, og_ref, gg_ref, gu_ref, gd_ref,
+def kernel(cfg, ids_ref, x_ref, dy_ref, wg_ref, wu_ref, wd_ref, og_v, gg_v, gu_v, gd_v,
            x_v, dy_v, w_gu, w_dn, shift_dy, shift_ids, g_a, g_b, x_all, dy_all, d_gu, hid, part,
-           s_r, r_r, s_l, r_l, s_y, r_y, og_v, gg_v, gu_v, gd_v,
+           s_r, r_r, s_l, r_l, s_y, r_y,
            loc, sh_s, sh_r, a1_s, a1_r, ar_s, ar_r, al_s, al_r, br_s, br_r, bl_s, bl_r, by_s, by_r,
            rr_s, rr_r, rl_s, rl_r, ry_s, ry_r):
     Y, Z, D, CA = cfg
@@ -299,14 +299,6 @@
         return 0
 
     lax.fori_loop(2, K, reduce_step, 0)
-    outs = [
-        pltpu.make_async_copy(gg_v, gg_ref, loc.at[0]),
-        pltpu.make_async_copy(gu_v, gu_ref, loc.at[1]),
-        pltpu.make_async_copy(gd_v, gd_ref, loc.at[2]),
-    ]
-    for copy in outs:
-        copy.start()
-
     def to_owner(j):
         yy = wrap(y + turn[j], Y)
         return remote(s_y.at[yy], r_y.at[j], ry_s.at[j], ry_r.at[j], owners[j])
@@ -334,8 +326,6 @@
         term = lax.dot_general(match, rows, ROWS_DIM, preferred_element_type=F32)
         cols = slice(cut * CW, (cut + 1) * CW)
         og_v[:, cols] = (shift_dy[:, cols].astype(F32) + term).astype(BF16)
-    last = pltpu.make_async_copy(og_v, og_ref, loc.at[3])
-    last.start()
 
     for copy in shift:
         copy.wait_send()
@@ -363,13 +353,15 @@
         return 0
 
     lax.fori_loop(0, K, sent, 0)
-    for copy in outs + [last]:
+
+
+def handout(*refs):
+    sems = refs[-1]
+    copies = [pltpu.make_async_copy(refs[i], refs[4 + i], sems.at[i]) for i in range(4)]
+    for copy in copies:
+        copy.start()
+    for copy in copies:
         copy.wait()
-
-
-def handout(*refs):
-    for source, target in zip(refs[:4], refs[4:]):
-        target[...] = source[...]
 
 
 def split(width):
@@ -394,30 +386,29 @@
         V((Z, CUTS, Y * SLOT, CW), F32),
         *[V((K, CUTS, Y * SLOT, CW), BF16)] * 4,
         *[V((Y, CUTS, 2 * SLOT, CW // 2), BF16)] * 2,
-        V((tokens, D), BF16), V((D, hidden), BF16), V((D, hidden), BF16), V((D, hidden), BF16),
         DMA((5,)), DMA((2,)), DMA((2,)), DMA((3,)), DMA((3,)),
         *[DMA((K, Y))] * 4, *[DMA((K,))] * 4, DMA((3, Z)), DMA((3, Z)),
         *[DMA((K, CUTS))] * 4, DMA((Y,)), DMA((Y,)),
     ]
     anywhere = pl.BlockSpec(memory_space=pl.ANY)
-    weight = jax.ShapeDtypeStruct((D, hidden), BF16)
-    token_grad, grad_gate, grad_up, grad_down = pl.pallas_call(
+    shapes = ((tokens, D), (D, hidden), (D, hidden), (D, hidden))
+    inside = pl.BlockSpec(memory_space=pltpu.VMEM)
+    made = pl.pallas_call(
         functools.partial(kernel, (Y, Z, D, CA)),
-        out_shape=(jax.ShapeDtypeStruct((tokens, D), BF16), weight, weight, weight),
-        in_specs=[pl.BlockSpec(memory_space=pltpu.VMEM)] + [anywhere] * 5,
-        out_specs=(anywhere,) * 4,
+        out_shape=tuple(V(shape, BF16) for shape in shapes),
+        in_specs=[inside] + [anywhere] * 5,
+        out_specs=(inside,) * 4,
         scratch_shapes=scratch,
-        compiler_params=pltpu.CompilerParams(collective_id=0, has_side_effects=True, vmem_limit_bytes=56 << 20),
+        compiler_params=pltpu.CompilerParams(collective_id=0, has_side_effects=True, vmem_limit_bytes=59 << 20),
     )(expert_ids, layer_input[0], output_grad[0], w_gate[0], w_up[0], w_down[0])
-    steps = 4
-    blocks = [pl.BlockSpec((n // steps, m), lambda i: (i, 0)) for n, m in ((tokens, D),) + ((D, hidden),) * 3]
     token_grad, grad_gate, grad_up, grad_down = pl.pallas_call(
         handout,
-        grid=(steps,),
-        out_shape=(jax.ShapeDtypeStruct((tokens, D), BF16), weight, weight, weight),
-        in_specs=blocks,
-        out_specs=blocks,
-    )(token_grad, grad_gate, grad_up, grad_down)
+        out_shape=tuple(jax.ShapeDtypeStruct(shape, BF16) for shape in shapes),
+        in_specs=[inside] * 4,
+        out_specs=(anywhere,) * 4,
+        scratch_shapes=[DMA((4,))],
+        compiler_params=pltpu.CompilerParams(vmem_limit_bytes=8 << 20),
+    )(*made)
     return token_grad[None], grad_gate[None], grad_up[None], grad_down[None]
 
 

time: 91.8 us -> 88.8 us (0.967)
  Pallas kernels: 91 us -> 88 us
    pallas_call x2, Pallas kernels: 91 us -> 88 us  [the longest x1 86.7 us: body(): pl.pallas_call(functools.partial(kernel, (Y, Z, D, CA)), out_shape=tuple(...]
where the time goes in v7:
time: 88.8 us; the launch traced here: 88.7 us
  Pallas kernels  88 us (99%)
    pallas_call x1, Pallas kernels, body(): pl.pallas_call(functools.partial(kernel, (Y, Z, D, CA)), out_shape=tuple(...  86.7 us

profile of v7, /device:TPU:1, one launch (start us, length us, event | category | flops | bytes accessed | tf_op | source)
XLA Modules:
  0.0 88.7 jit_solution(7865644553295222407)
XLA Ops:
  0.6 86.7 %shard_map.93 = (bf16[128,2048]{1,0:T(8,128)(2,1)S(1)}, bf16[2048,128]{1,0:T(8,128)(2,1)S(1)}, bf16[2048,128]{1,0:T(8,128)(2,1)S(1)}, bf16[2048,128]{1,0:T(8,128)(2,1)S(1)}) custom-call(s32[1,128]{1,0:T(1,128)} %ids_ref.1, bf16[128,2048]{1,0:T(8,128)(2,1)} %bitcast.9, bf16[128,2048]{1,0:T(8,128)(2,1)} %bitcast.10, bf16[2048,128]{1,0:T(8,128)(2,1)} %bitcast.11, ...), custom_call_target="tpu_custom_call" | custom-call | tf_op jit(solution)/shard_map/pallas_call | solution.py:396
  87.3 1.3 %shard_map.94 = (bf16[128,2048]{1,0:T(8,128)(2,1)}, bf16[2048,128]{1,0:T(8,128)(2,1)}, bf16[2048,128]{1,0:T(8,128)(2,1)}, bf16[2048,128]{1,0:T(8,128)(2,1)}) custom-call(bf16[128,2048]{1,0:T(8,128)(2,1)S(1)} %get-tuple-element.12.refs_0_, bf16[2048,128]{1,0:T(8,128)(2,1)S(1)} %get-tuple-element.13.refs_1_, bf16[2048,128]{1,0:T(8,128)(2,1)S(1)} %get-tuple-element.14.refs_2_, ...), custom_call_target="tpu_custom_call" | custom-call | tf_op jit(solution)/shard_map/pallas_call | solution.py:404

commit v8 on v7

--- a/solution.py
+++ b/solution.py
@@ -299,26 +299,28 @@
         return 0
 
     lax.fori_loop(2, K, reduce_step, 0)
-    def to_owner(j):
+    def to_owner(group, j):
+        cuts = pl.ds(group * (CUTS // 2), CUTS // 2)
         yy = wrap(y + turn[j], Y)
-        return remote(s_y.at[yy], r_y.at[j], ry_s.at[j], ry_r.at[j], owners[j])
-
-    for a, b in zip(list(second) + list(first), list(first) + list(second)):
-        to_right(K - 1, a).wait_recv()
-        to_left(K - 1, b).wait_recv()
-    for cut in range(CUTS):
+        return remote(s_y.at[yy, cuts], r_y.at[j, cuts], ry_s.at[group, j], ry_r.at[group, j], owners[j])
+
+    for copy in shift:
+        copy.wait_recv()
+    match = slot_match(shift_ids[...])
+    for cut in list(second) + list(first):
+        to_right(K - 1, cut).wait_recv()
+        to_left(K - 1, cut).wait_recv()
         total = part[0, cut] + r_r[K - 1, cut].astype(F32) + r_l[K - 1, cut].astype(F32)
         total = total.reshape(Y, SLOT, CW)
         total = jnp.concatenate([total[:, :, :CW // 2], total[:, :, CW // 2:]], axis=1).astype(BF16)
         s_y[:, cut] = total
-    for j in (3, 1, 2, 0):
-        to_owner(j).start()
-    for copy in shift:
-        copy.wait_recv()
-    match = slot_match(shift_ids[...])
-    for j in range(Y):
-        to_owner(j).wait_recv()
-    for cut in range(CUTS):
+        if cut in (second[-1], first[-1]):
+            for j in (3, 1, 2, 0):
+                to_owner(1 if cut in second else 0, j).start()
+    for cut in list(second) + list(first):
+        if cut in (second[0], first[0]):
+            for j in range(Y):
+                to_owner(1 if cut in second else 0, j).wait_recv()
         rows = r_y[0, cut].astype(F32)
         for j in range(1, Y):
             rows = rows + r_y[j, cut].astype(F32)
@@ -332,7 +334,8 @@
     for j, to in enumerate((y_right, y_left, y_far)):
         a1(j, to).wait_send()
     for j in range(Y):
-        to_owner(j).wait_send()
+        to_owner(0, j).wait_send()
+        to_owner(1, j).wait_send()
 
     def sent(k, _):
         for j in range(Y):
@@ -388,7 +391,7 @@
         *[V((Y, CUTS, 2 * SLOT, CW // 2), BF16)] * 2,
         DMA((5,)), DMA((2,)), DMA((2,)), DMA((3,)), DMA((3,)),
         *[DMA((K, Y))] * 4, *[DMA((K,))] * 4, DMA((3, Z)), DMA((3, Z)),
-        *[DMA((K, CUTS))] * 4, DMA((Y,)), DMA((Y,)),
+        *[DMA((K, CUTS))] * 4, DMA((2, Y)), DMA((2, Y)),
     ]
     anywhere = pl.BlockSpec(memory_space=pl.ANY)
     shapes = ((tokens, D), (D, hidden), (D, hidden), (D, hidden))

time: 88.8 us -> 88.6 us (level)
  no operation moved by 1% of the time
where the time goes in v8:
time: 88.6 us; the launch traced here: 88.5 us
  Pallas kernels  87.8 us (99%)
    pallas_call x1, Pallas kernels, body(): pl.pallas_call(functools.partial(kernel, (Y, Z, D, CA)), out_shape=tuple(...  86.5 us

profile of v8, /device:TPU:1, one launch (start us, length us, event | category | flops | bytes accessed | tf_op | source)
XLA Modules:
  0.0 88.5 jit_solution(5089519769538049465)
XLA Ops:
  0.6 86.5 %shard_map.93 = (bf16[128,2048]{1,0:T(8,128)(2,1)S(1)}, bf16[2048,128]{1,0:T(8,128)(2,1)S(1)}, bf16[2048,128]{1,0:T(8,128)(2,1)S(1)}, bf16[2048,128]{1,0:T(8,128)(2,1)S(1)}) custom-call(s32[1,128]{1,0:T(1,128)} %ids_ref.1, bf16[128,2048]{1,0:T(8,128)(2,1)} %bitcast.9, bf16[128,2048]{1,0:T(8,128)(2,1)} %bitcast.10, bf16[2048,128]{1,0:T(8,128)(2,1)} %bitcast.11, ...), custom_call_target="tpu_custom_call" | custom-call | tf_op jit(solution)/shard_map/pallas_call | solution.py:399
  87.1 1.3 %shard_map.94 = (bf16[128,2048]{1,0:T(8,128)(2,1)}, bf16[2048,128]{1,0:T(8,128)(2,1)}, bf16[2048,128]{1,0:T(8,128)(2,1)}, bf16[2048,128]{1,0:T(8,128)(2,1)}) custom-call(bf16[128,2048]{1,0:T(8,128)(2,1)S(1)} %get-tuple-element.12.refs_0_, bf16[2048,128]{1,0:T(8,128)(2,1)S(1)} %get-tuple-element.13.refs_1_, bf16[2048,128]{1,0:T(8,128)(2,1)S(1)} %get-tuple-element.14.refs_2_, ...), custom_call_target="tpu_custom_call" | custom-call | tf_op jit(solution)/shard_map/pallas_call | solution.py:407
